TPU v7x, 32 devices: a whole 2x2x4 slice. The times are simulated.
32 devices in a mesh: row: 16 (over z, x, core), col: 2 (over y).
Axes of the slice: x: 2, y: 2, z: 4, core: 2. Of those that a mesh axis runs over, the one named last changes fastest.
Arguments:
- eigvecs: float32 [4096, 2048], P('row', 'col'), may hold values from -6 to 6
- panels: float32 [5, 16, 256, 128], P(None, 'row', 'col'), may hold values from -6 to 6
- sweep_shift: int32 [5], replicated, may hold values from 0 to 15
- slot_group: int32 [5, 16], replicated, may hold values from 0 to 15, each once within a row
Outputs:
- full_vectors: float32 [4096, 2048], P('row', 'col')
Inputs may be any that keep to these rules, and one draw needn't show every extreme that they name: Each row of slot_group names each of the 16 groups once.
All inputs are finite; a program needn't handle non-finite values.
Results may differ from a plain program's by a relative error of at most 0.00029.
Values sent between devices are 32-bit elements; how exact they have to be, the bound alone decides.
No kernel may reach another device: no remote copies, remote signals or barrier semaphores. Data moves between devices by JAX's collectives and lax.ppermute only.
A program may use at most 128 MiB of HBM per device.

v0:
```python
import functools

import jax
import jax.numpy as jnp
from jax import lax
from jax.experimental import pallas as pl
from jax.experimental.pallas import tpu as pltpu
from jax.sharding import PartitionSpec as P

F32 = jnp.float32
BF16 = jnp.bfloat16
FULL = lax.Precision.HIGHEST
VMEM_LIMIT = 48 * 1024 * 1024


def dot_full(a, b):
    return jnp.dot(a, b, precision=FULL, preferred_element_type=F32)


def halves(x):
    high = x.astype(BF16)
    low = (x - high.astype(F32)).astype(BF16)
    return high, low


def dot_split(a, b):
    a_high, a_low = a
    b_high, b_low = b
    total = jnp.dot(a_high, b_low, preferred_element_type=F32)
    total += jnp.dot(a_low, b_high, preferred_element_type=F32)
    return total + jnp.dot(a_high, b_high, preferred_element_type=F32)


def inverse_factors(grams):
    order = grams[0].shape[0]
    row = lax.broadcasted_iota(jnp.int32, (order, order), 0)
    col = lax.broadcasted_iota(jnp.int32, (order, order), 1)
    diagonal = row == col

    def corner(width):
        same = (row // (2 * width)) == (col // (2 * width))
        return same & ((row // width) % 2 == 0) & ((col // width) % 2 == 1)

    results = []
    for gram in grams:
        kept = jnp.where(diagonal, gram, 0.0)
        inv_col = 2.0 / jnp.sum(kept, axis=1, keepdims=True)
        inv_row = 2.0 / jnp.sum(kept, axis=0, keepdims=True)
        first = jnp.where(corner(1), gram * inv_col * inv_row, 0.0)
        results.append(jnp.where(diagonal, jnp.broadcast_to(inv_row, gram.shape), 0.0) - first)
    width = 2
    while width < order:
        mask = corner(width)
        inner = [dot_full(x, jnp.where(mask, g, 0.0)) for x, g in zip(results, grams)]
        results = [x - dot_full(i, x) for x, i in zip(results, inner)]
        width *= 2
    return results


def reorder_kernel(shift_ref, group_ref, pieces_ref, out_ref):
    slots, sweeps = pieces_ref.shape[:2]
    cols = out_ref.shape[1]

    def one_slot(slot, carry):
        for sweep in range(sweeps):
            window = lax.rem(group_ref[sweep, slot] + shift_ref[sweep], slots)
            piece = pieces_ref[slot, sweep]
            for c in range(cols):
                out_ref[window, c, sweep] = piece
            if sweep % 2 == 1:
                after = lax.rem(window + 1, slots)
                for c in range(cols):
                    out_ref[after, c, sweeps + sweep // 2] = piece
        return carry

    lax.fori_loop(0, slots, one_slot, 0)


def fetch_panel(recv_ref, block):
    rows, cols, _, piece, band = recv_ref.shape
    parts = [recv_ref[q, c, block] for c in range(cols) for q in range(rows)]
    return jnp.concatenate(parts, axis=0)


def first_kernel(parity_ref, recv_ref, z_ref, core_ref, pair_ref, a_ref):
    half = core_ref.shape[0]
    panel = fetch_panel(recv_ref, 0)
    panel_t = panel.T
    gram = dot_full(panel_t, panel)
    projected = dot_split(halves(panel_t), halves(z_ref[...]))
    (inverse,) = inverse_factors([gram])
    a_ref[...] = dot_full(panel, inverse)
    projected = halves(projected)
    parity = parity_ref[0]
    for out_ref, start in ((core_ref, (1 - parity) * half), (pair_ref, parity * half)):
        rows = pl.ds(pl.multiple_of(start, half), half)
        out_ref[...] = z_ref[rows, :] - dot_split(halves(a_ref[rows, :]), projected)


def arranged(parity, natural):
    before, top, bottom, after = natural
    even = parity == 0
    return [
        jnp.where(even, after, before),
        jnp.where(even, before, after),
        jnp.where(even, bottom, top),
        jnp.where(even, top, bottom),
    ]


def operator_kernel(parity_ref, recv_ref, high1_ref, low1_ref, high2_ref, low2_ref):
    parity = parity_ref[0]
    numbers = (1, 5, 2, 3, 6, 4)
    panels = [fetch_panel(recv_ref, number) for number in numbers]
    panels_t = [p.T for p in panels]
    half = panels[0].shape[0] // 2
    inverses = inverse_factors([dot_full(t, p) for t, p in zip(panels_t, panels)])
    size = 2 * half
    row = lax.broadcasted_iota(jnp.int32, (size, size), 0)
    col = lax.broadcasted_iota(jnp.int32, (size, size), 1)
    identity = jnp.where(row == col, 1.0, 0.0).astype(F32)
    lead = (slice(0, half), slice(half, size), slice(0, size)) * 2
    operators = []
    for panel, panel_t, inverse, rows in zip(panels, panels_t, inverses, lead):
        scaled = dot_full(panel[rows], inverse)
        operators.append(identity[rows] - dot_full(scaled, panel_t))
    for number, high_ref, low_ref in ((0, high1_ref, low1_ref), (3, high2_ref, low2_ref)):
        own, other, last = operators[number : number + 3]
        left = dot_full(last[:, :half], other)
        right = dot_full(last[:, half:], own)
        natural = (left[:, :half], left[:, half:], right[:, :half], right[:, half:])
        merged = jnp.concatenate(arranged(parity, natural), axis=1)
        if number == 0:
            even = parity == 0
            upper, lower = merged[:half], merged[half:]
            merged = jnp.concatenate([jnp.where(even, lower, upper), jnp.where(even, upper, lower)], axis=0)
        high_ref[...], low_ref[...] = halves(merged)


def apply_kernel(high_ref, low_ref, *refs):
    inputs, outputs = refs[:4], refs[4:]
    stacked = jnp.concatenate([ref[...] for ref in inputs], axis=0)
    total = dot_split((high_ref[...], low_ref[...]), halves(stacked))
    at = 0
    for ref in outputs:
        ref[...] = total[at : at + ref.shape[0]]
        at += ref.shape[0]


def call(kernel, in_spaces, outs, scratch=()):
    return pl.pallas_call(
        kernel,
        in_specs=[pl.BlockSpec(memory_space=space) for space in in_spaces],
        out_specs=[pl.BlockSpec(memory_space=pltpu.VMEM) for _ in outs],
        out_shape=[jax.ShapeDtypeStruct(shape, dtype) for shape, dtype in outs],
        scratch_shapes=list(scratch),
        compiler_params=pltpu.CompilerParams(vmem_limit_bytes=VMEM_LIMIT),
    )


def on_device(eigvecs, panels, sweep_shift, slot_group):
    sweeps, _, panel_rows, band = panels.shape
    rows_dev, cols_dev = eigvecs.shape
    half = rows_dev // 2
    row_count, col_count = lax.axis_size("row"), lax.axis_size("col")
    piece = panel_rows // row_count
    smem, vmem = pltpu.SMEM, pltpu.VMEM
    parity = (lax.axis_index("row") % 2).astype(jnp.int32).reshape(1)

    split = panels.reshape(sweeps, row_count, piece, band).transpose(1, 0, 2, 3)
    pieces = lax.all_to_all(split, "row", 0, 0, tiled=True)
    blocks = sweeps + sweeps // 2
    routed_shape = (row_count, col_count, blocks, piece, band)
    (routed,) = call(reorder_kernel, (smem, smem, vmem), [(routed_shape, F32)])(sweep_shift, slot_group, pieces)
    recv = lax.all_to_all(routed.reshape(row_count * col_count, blocks, piece, band), ("row", "col"), 0, 0, tiled=True)
    recv = recv.reshape(routed_shape)

    core_route = [(i, i ^ 1) for i in range(row_count)]
    pair_route = [(i, (i + 1 if i % 2 else i - 1) % row_count) for i in range(row_count)]
    block = ((half, cols_dev), F32)
    own = call(first_kernel, (smem, vmem, vmem), [block, block], [pltpu.VMEM((rows_dev, band), F32)])(parity, recv, eigvecs)
    weight = ((rows_dev, 2 * rows_dev), BF16)
    high1, low1, high2, low2 = call(operator_kernel, (smem, vmem), [weight] * 4)(parity, recv)
    for high, low, outs in ((high1, low1, [block, block]), (high2, low2, [((rows_dev, cols_dev), F32)])):
        from_core = lax.ppermute(own[0], "row", core_route)
        from_pair = lax.ppermute(own[1], "row", pair_route)
        own = call(apply_kernel, (vmem,) * 6, outs)(high, low, from_core, from_pair, *own)
    return own[0]


def solution(mesh):
    in_specs = (P("row", "col"), P(None, "row", "col", None), P(), P())
    return jax.shard_map(on_device, mesh=mesh, in_specs=in_specs, out_specs=P("row", "col"), check_vma=False)
```

profile of v0, /device:TPU:1, one launch (start us, length us, event | category | flops | bytes accessed | tf_op | source)
XLA Modules:
  0.0 83.5 jit_solution(2565229860109901957)
XLA Ops:
  0.0 0.0 copy-start
  0.0 1.0 %copy-done = f32[5,1,128,128]{3,2,1,0:T(8,128)S(1)} copy-done((f32[5,1,128,128]{3,2,1,0:T(8,128)S(1)}, f32[5,1,128,128]{3,2,1,0:T(8,128)}, u32[]{:S(2)}) %copy-start) | copy-done | bytes 327704
  1.0 0.0 copy-start.2
  1.0 0.0 copy-start.3
  1.0 17.9 %all_to_all.10.pieces_ref = f32[16,5,8,128]{3,2,1,0:T(8,128)S(1)} all-to-all(f32[16,5,8,128]{3,2,1,0:T(8,128)S(1)} %copy_bitcast_fusion), channel_id=1, replica_groups=mesh['row'=16,'col'=2] {'row'}, dimensions={0} | all-to-all | bytes 655360 | tf_op jit(solution)/shard_map/all_to_all | solution.py:171
  18.9 0.0 copy-done.2
  18.9 0.0 copy-done.3
  18.9 2.0 %shard_map.46 = f32[16,2,7,8,128]{4,3,2,1,0:T(8,128)} custom-call(s32[5]{0:T(128)S(1)} %copy-done.3, s32[5,16]{1,0:T(8,128)S(1)} %copy-done.2, f32[16,5,8,128]{3,2,1,0:T(8,128)S(1)} %all_to_all.10.pieces_ref), custom_call_target="tpu_custom_call" | custom-call | tf_op jit(solution)/shard_map/pallas_call | solution.py:174
  20.9 0.0 copy-start.1
  20.9 3.3 %all-to-all-start.1 = ((f32[32,7,8,128]{3,2,1,0:T(8,128)}), f32[32,7,8,128]{3,2,1,0:T(8,128)S(1)}, u32[]{:S(2)}, u32[]{:S(2)}) async-start(f32[32,7,8,128]{3,2,1,0:T(8,128)} %bitcast.3), calls=%async_computation.1 | async-start | bytes 1835008 | tf_op jit(solution)/shard_map/all_to_all | solution.py:175
  24.3 23.4 %all-to-all-done.1 = f32[32,7,8,128]{3,2,1,0:T(8,128)S(1)} async-done(((f32[32,7,8,128]{3,2,1,0:T(8,128)}), f32[32,7,8,128]{3,2,1,0:T(8,128)S(1)}, u32[]{:S(2)}, u32[]{:S(2)}) %all-to-all-start.1) | async-done | bytes 917536 | tf_op jit(solution)/shard_map/all_to_all | solution.py:175
  47.7 0.0 copy-done.1
  47.7 3.8 %shard_map.48 = (f32[128,1024]{1,0:T(8,128)S(1)}, f32[128,1024]{1,0:T(8,128)S(1)}) custom-call(s32[1]{0:T(128)} %bitcast.parity_ref, f32[16,2,7,8,128]{4,3,2,1,0:T(8,128)S(1)} %bitcast.8, f32[256,1024]{1,0:T(8,128)S(1)} %copy-done.1), custom_call_target="tpu_custom_call" | custom-call | tf_op jit(solution)/shard_map/pallas_call | solution.py:181
  51.5 0.3 collective-permute-start
  51.8 1.5 %collective-permute-start.1 = (f32[128,1024]{1,0:T(8,128)S(1)}, f32[128,1024]{1,0:T(8,128)S(1)}, u32[]{:S(2)}, u32[]{:S(2)}) collective-permute-start(f32[128,1024]{1,0:T(8,128)S(1)} %get-tuple-element.18.refs_3_), channel_id=1, source_target_pairs={{0,30},{2,4},{4,2},{6,8},{8,6},{10,12},{12,10},{14,16},{16,14},{18... | collective-permute-start | bytes 1572872 | tf_op jit(solution)/shard_map/ppermute | solution.py:186
  53.3 8.3 %shard_map.47 = (bf16[256,512]{1,0:T(8,128)(2,1)S(1)}, bf16[256,512]{1,0:T(8,128)(2,1)S(1)}, bf16[256,512]{1,0:T(8,128)(2,1)S(1)}, bf16[256,512]{1,0:T(8,128)(2,1)S(1)}) custom-call(s32[1]{0:T(128)} %bitcast.parity_ref, f32[16,2,7,8,128]{4,3,2,1,0:T(8,128)S(1)} %bitcast.9), custom_call_target="tpu_custom_call" | custom-call | tf_op jit(solution)/shard_map/pallas_call | solution.py:183
  61.6 0.0 collective-permute-done.refs_0_
  61.6 4.5 %collective-permute-done.1.refs_1_ = f32[128,1024]{1,0:T(8,128)S(1)} collective-permute-done((f32[128,1024]{1,0:T(8,128)S(1)}, f32[128,1024]{1,0:T(8,128)S(1)}, u32[]{:S(2)}, u32[]{:S(2)}) %collective-permute-start.1) | collective-permute-done | bytes 524320 | tf_op jit(solution)/shard_map/ppermute | solution.py:186
  66.1 1.0 %shard_map.49 = (f32[128,1024]{1,0:T(8,128)S(1)}, f32[128,1024]{1,0:T(8,128)S(1)}) custom-call(bf16[256,512]{1,0:T(8,128)(2,1)S(1)} %get-tuple-element.15.high_ref, bf16[256,512]{1,0:T(8,128)(2,1)S(1)} %get-tuple-element.16.low_ref, f32[128,1024]{1,0:T(8,128)S(1)} %collective-permute-done.refs_0_, f32[128,1024]{1,0:T(8,128)S(1)} %collective-permute-done.1.refs_1_, ...), custom_call_target="tpu_custom_call" | custom-call | tf_op jit(solution)/shard_map/pallas_call | solution.py:187
  67.1 0.1 collective-permute-start.2
  67.2 1.6 %collective-permute-start.3 = (f32[128,1024]{1,0:T(8,128)S(1)}, f32[128,1024]{1,0:T(8,128)S(1)}, u32[]{:S(2)}, u32[]{:S(2)}) collective-permute-start(f32[128,1024]{1,0:T(8,128)S(1)} %get-tuple-element.20.refs_3_), channel_id=1, source_target_pairs={{0,30},{2,4},{4,2},{6,8},{8,6},{10,12},{12,10},{14,16},{16,14},{18... | collective-permute-start | bytes 1572872 | tf_op jit(solution)/shard_map/ppermute | solution.py:186
  68.8 0.3 collective-permute-done.2.refs_0_
  69.1 12.4 %collective-permute-done.3.refs_1_ = f32[128,1024]{1,0:T(8,128)S(1)} collective-permute-done((f32[128,1024]{1,0:T(8,128)S(1)}, f32[128,1024]{1,0:T(8,128)S(1)}, u32[]{:S(2)}, u32[]{:S(2)}) %collective-permute-start.3) | collective-permute-done | bytes 524320 | tf_op jit(solution)/shard_map/ppermute | solution.py:186
  81.5 2.0 %shard_map.50 = f32[256,1024]{1,0:T(8,128)} custom-call(bf16[256,512]{1,0:T(8,128)(2,1)S(1)} %get-tuple-element.13.high_ref, bf16[256,512]{1,0:T(8,128)(2,1)S(1)} %get-tuple-element.14.low_ref, f32[128,1024]{1,0:T(8,128)S(1)} %collective-permute-done.2.refs_0_, f32[128,1024]{1,0:T(8,128)S(1)} %collective-permute-done.3.refs_1_, ...), custom_call_target="tpu_custom_call" | custom-call | tf_op jit(solution)/shard_map/pallas_call | solution.py:187
  (1 shorter events, 0.0 us)
Async XLA Ops:
  0.0 1.0 %copy-start = (f32[5,1,128,128]{3,2,1,0:T(8,128)S(1)}, f32[5,1,128,128]{3,2,1,0:T(8,128)}, u32[]{:S(2)}) copy-start(f32[5,1,128,128]{3,2,1,0:T(8,128)} %param.5) | copy-start | bytes 983044
  1.0 17.9 %copy-start.2 = (s32[5,16]{1,0:T(8,128)S(1)}, s32[5,16]{1,0:T(8,128)}, u32[]{:S(2)}) copy-start(s32[5,16]{1,0:T(8,128)} %group_ref.1) | copy-start | bytes 964
  1.0 17.9 %copy-start.3 = (s32[5]{0:T(128)S(1)}, s32[5]{0:T(128)}, u32[]{:S(2)}) copy-start(s32[5]{0:T(128)} %shift_ref.1) | copy-start | bytes 64
  20.9 26.8 %copy-start.1 = (f32[256,1024]{1,0:T(8,128)S(1)}, f32[256,1024]{1,0:T(8,128)}, u32[]{:S(2)}) copy-start(f32[256,1024]{1,0:T(8,128)} %z_ref.1) | copy-start | bytes 3145732
  20.9 26.8 %all-to-all-start.1 = ((f32[32,7,8,128]{3,2,1,0:T(8,128)}), f32[32,7,8,128]{3,2,1,0:T(8,128)S(1)}, u32[]{:S(2)}, u32[]{:S(2)}) async-start(f32[32,7,8,128]{3,2,1,0:T(8,128)} %bitcast.3), calls=%async_computation.1 | async-start | bytes 1835008 | tf_op jit(solution)/shard_map/all_to_all | solution.py:175
  51.5 10.1 %collective-permute-start = (f32[128,1024]{1,0:T(8,128)S(1)}, f32[128,1024]{1,0:T(8,128)S(1)}, u32[]{:S(2)}, u32[]{:S(2)}) collective-permute-start(f32[128,1024]{1,0:T(8,128)S(1)} %get-tuple-element.17.refs_2_), channel_id=1, source_target_pairs={{0,2},{2,0},{4,6},{6,4},{8,10},{10,8},{12,14},{14,12},{16,18},{18,... | collective-permute-start | bytes 1572872 | tf_op jit(solution)/shard_map/ppermute | solution.py:185
  51.8 14.2 %collective-permute-start.1 = (f32[128,1024]{1,0:T(8,128)S(1)}, f32[128,1024]{1,0:T(8,128)S(1)}, u32[]{:S(2)}, u32[]{:S(2)}) collective-permute-start(f32[128,1024]{1,0:T(8,128)S(1)} %get-tuple-element.18.refs_3_), channel_id=1, source_target_pairs={{0,30},{2,4},{4,2},{6,8},{8,6},{10,12},{12,10},{14,16},{16,14},{18... | collective-permute-start | bytes 1572872 | tf_op jit(solution)/shard_map/ppermute | solution.py:186
  67.1 2.0 %collective-permute-start.2 = (f32[128,1024]{1,0:T(8,128)S(1)}, f32[128,1024]{1,0:T(8,128)S(1)}, u32[]{:S(2)}, u32[]{:S(2)}) collective-permute-start(f32[128,1024]{1,0:T(8,128)S(1)} %get-tuple-element.19.refs_2_), channel_id=1, source_target_pairs={{0,2},{2,0},{4,6},{6,4},{8,10},{10,8},{12,14},{14,12},{16,18},{18,... | collective-permute-start | bytes 1572872 | tf_op jit(solution)/shard_map/ppermute | solution.py:185
  67.2 14.3 %collective-permute-start.3 = (f32[128,1024]{1,0:T(8,128)S(1)}, f32[128,1024]{1,0:T(8,128)S(1)}, u32[]{:S(2)}, u32[]{:S(2)}) collective-permute-start(f32[128,1024]{1,0:T(8,128)S(1)} %get-tuple-element.20.refs_3_), channel_id=1, source_target_pairs={{0,30},{2,4},{4,2},{6,8},{8,6},{10,12},{12,10},{14,16},{16,14},{18... | collective-permute-start | bytes 1572872 | tf_op jit(solution)/shard_map/ppermute | solution.py:186
where the time goes:
time: 83.7 us; the launch traced here: 83.5 us
  waiting for transfers between devices  40.6 us (49%)
  blocking collectives  17.9 us (21%)
  Pallas kernels  17.1 us (20%)
  starting transfers between devices  6.75 us (8%)
  local copies, waits for them, and re-layouts  1.01 us (1%)
    all_to_all x1, waiting for transfers between devices, on_device(): lax.all_to_all(routed.reshape(row_count * col_count, blocks, piece, band)...  23.4 us
    all_to_all x1, blocking collectives, on_device(): pieces = lax.all_to_all(split, 'row', 0, 0, tiled=True)  17.9 us
    ppermute x2, waiting for transfers between devices, on_device(): from_pair = lax.ppermute(own[1], 'row', pair_route)  16.8 us
    pallas_call x1, Pallas kernels, on_device(): call(operator_kernel, (smem, vmem), [weight] * 4)(parity, recv)  8.26 us
    pallas_call x1, Pallas kernels, on_device(): call(first_kernel, (smem, vmem, vmem), [block, block], [pltpu.VMEM((rows_...  3.83 us
    all_to_all x1, starting transfers between devices, on_device(): lax.all_to_all(routed.reshape(row_count * col_count, blocks, piece, band)...  3.32 us
    ppermute x2, starting transfers between devices, on_device(): from_pair = lax.ppermute(own[1], 'row', pair_route)  3.06 us
    pallas_call x2, Pallas kernels, on_device(): call(apply_kernel, (vmem,) * 6, outs)(high, low, from_core, from_pair, *own)  3.01 us
  transfers between devices with their start and end apart: 5, of which 4 were waited for; matrix products, arithmetic and copies ran while one was open for 0% of the time, Pallas kernels for 10%

commit v1 on v0

v1 whole, which is shorter than its diff:
```python
import functools

import jax
import jax.numpy as jnp
from jax import lax
from jax.experimental import pallas as pl
from jax.experimental.pallas import tpu as pltpu
from jax.sharding import PartitionSpec as P

F32 = jnp.float32
BF16 = jnp.bfloat16
VMEM_LIMIT = 48 * 1024 * 1024


def mxu(a, b):
    return jnp.dot(a, b, preferred_element_type=F32)


def beside(*blocks):
    return jnp.concatenate(blocks, axis=1)


def above(*blocks):
    return jnp.concatenate(blocks, axis=0)


def halves(x):
    high = x.astype(BF16)
    low = (x - high.astype(F32)).astype(BF16)
    return high, low


def thirds(x):
    high = x.astype(BF16)
    rest = x - high.astype(F32)
    middle = rest.astype(BF16)
    return high, middle, (rest - middle.astype(F32)).astype(BF16)


def dot_full(a, b):
    a_high, a_middle, a_low = thirds(a)
    b_high, b_middle, b_low = thirds(b)
    depth, width = b.shape
    small = mxu(beside(a_high, a_low), above(b_low, b_high))
    if depth > 128:
        large = mxu(a_high, beside(b_high, b_middle))
        large += mxu(a_middle, beside(b_high, b_middle))
    elif width > 128:
        left = beside(a_high, a_middle)
        return small + mxu(left, above(b_middle, b_middle)) + mxu(left, above(b_high, b_high))
    else:
        right = beside(b_high, b_middle)
        large = mxu(beside(a_high, a_middle), above(right, right))
    return small + large[:, width:] + large[:, :width]


def dot_split(a, b):
    a_high, a_low = a
    b_high, b_low = b
    if b_high.shape[0] > 128:
        return mxu(a_high, b_low) + mxu(a_low, b_high) + mxu(a_high, b_high)
    return mxu(a_high, b_low) + mxu(beside(a_high, a_low), above(b_high, b_high))


def inverse_factors(grams):
    order = grams[0].shape[0]
    row = lax.broadcasted_iota(jnp.int32, (order, order), 0)
    col = lax.broadcasted_iota(jnp.int32, (order, order), 1)
    diagonal = row == col

    def corner(width):
        same = (row // (2 * width)) == (col // (2 * width))
        return same & ((row // width) % 2 == 0) & ((col // width) % 2 == 1)

    results = []
    for gram in grams:
        kept = jnp.where(diagonal, gram, 0.0)
        inv_col = 2.0 / jnp.sum(kept, axis=1, keepdims=True)
        inv_row = 2.0 / jnp.sum(kept, axis=0, keepdims=True)
        first = jnp.where(corner(1), gram * inv_col * inv_row, 0.0)
        results.append(jnp.where(diagonal, jnp.broadcast_to(inv_row, gram.shape), 0.0) - first)
    width = 2
    while width < order:
        if 4 * width <= order:
            mask = ((row // (4 * width)) == (col // (4 * width))) & ((row // width) < (col // width))
            inner = [dot_full(x, jnp.where(mask, g, 0.0)) for x, g in zip(results, grams)]
            squares = [dot_full(n, n) for n in inner]
            once = [x - dot_full(n, x) for x, n in zip(results, inner)]
            results = [y + dot_full(n, y) for y, n in zip(once, squares)]
            width *= 4
        else:
            mask = corner(width)
            inner = [dot_full(x, jnp.where(mask, g, 0.0)) for x, g in zip(results, grams)]
            results = [x - dot_full(n, x) for x, n in zip(results, inner)]
            width *= 2
    return results


def wrapped(index, size):
    return jnp.where(index >= size, index - size, index)


def reorder_kernel(layout, shift_ref, group_ref, pieces_ref, out_ref, buffer, sem):
    slots = pieces_ref.shape[0]
    for slot in range(slots):
        for sweep, targets in enumerate(layout):
            window = wrapped(group_ref[sweep, slot] + shift_ref[sweep], slots)
            piece = pieces_ref[slot, sweep]
            for block, columns, distance in targets:
                target = wrapped(window + 1, slots) if distance else window
                for c in columns:
                    buffer[target, c, block] = piece
    copy = pltpu.make_async_copy(buffer, out_ref, sem)
    copy.start()
    copy.wait()


def fetch_panel(recv_ref, *index):
    rows, cols = recv_ref.shape[:2]
    parts = [recv_ref[(q, c) + index] for c in range(cols) for q in range(rows)]
    return jnp.concatenate(parts, axis=0)


def first_kernel(groups, place_ref, recv_ref, z_ref, core_ref, pair_ref, *refs):
    half = core_ref.shape[0]
    a_ref, sem = refs[-2:]
    copies = []
    for blocks, ref in zip(groups, refs[:-2]):
        for number, block in enumerate(blocks):
            copies.append(pltpu.make_async_copy(recv_ref.at[:, :, block], ref.at[:, :, number], sem.at[len(copies)]))
            copies[-1].start()
    panel = fetch_panel(recv_ref, 0)
    panel_t = panel.T
    gram = dot_full(panel_t, panel)
    projected = halves(dot_split(halves(panel_t), halves(z_ref[...])))
    (inverse,) = inverse_factors([gram])
    a_ref[...] = dot_full(panel, inverse)
    parity = place_ref[0]
    for out_ref, start in ((core_ref, (1 - parity) * half), (pair_ref, parity * half)):
        rows = pl.ds(pl.multiple_of(start, half), half)
        out_ref[...] = z_ref[rows, :] - dot_split(halves(a_ref[rows, :]), projected)
    for copy in copies:
        copy.wait()


def arranged(parity, natural):
    before, top, bottom, after = natural
    even = parity == 0
    return [
        jnp.where(even, before, after),
        jnp.where(even, after, before),
        jnp.where(even, bottom, top),
        jnp.where(even, top, bottom),
    ]


def operator_kernel(odd, even, for_exchange, place_ref, *refs):
    sources, (core_in, core_own, pair_own, partial_ref, high_ref, low_ref) = refs[:-6], refs[-6:]
    parity, column = place_ref[0], place_ref[1]

    def panel_of(choices):
        chosen = [fetch_panel(sources[source], block) for source, block in choices]
        return chosen[0] if len(chosen) == 1 else jnp.where(column == 0, chosen[0], chosen[1])

    panels = [panel_of(choices) for choices in (*odd, even)]
    panels_t = [p.T for p in panels]
    size = panels[0].shape[0]
    half = size // 2
    inverses = inverse_factors([dot_full(t, p) for t, p in zip(panels_t, panels)])
    row = lax.broadcasted_iota(jnp.int32, (size, size), 0)
    col = lax.broadcasted_iota(jnp.int32, (size, size), 1)
    identity = jnp.where(row == col, 1.0, 0.0).astype(F32)
    operators = []
    for panel, panel_t, inverse, rows in zip(panels, panels_t, inverses, (slice(0, half), slice(half, size), slice(0, size))):
        scaled = dot_full(panel[rows], inverse)
        operators.append(identity[rows] - dot_full(scaled, panel_t))
    own, other, last = operators
    if for_exchange:
        flipped = parity == 0
        upper, lower = last[:half], last[half:]
        last = jnp.concatenate([jnp.where(flipped, lower, upper), jnp.where(flipped, upper, lower)], axis=0)
    left = dot_split(halves(last[:, :half]), halves(other))
    right = dot_split(halves(last[:, half:]), halves(own))
    natural = (left[:, :half], left[:, half:], right[:, :half], right[:, half:])
    first, *rest = arranged(parity, natural)
    high_ref[...], low_ref[...] = halves(first)
    rows = jnp.concatenate([core_in[...], core_own[...], pair_own[...]], axis=0)
    partial_ref[...] = dot_split(halves(jnp.concatenate(rest, axis=1)), halves(rows))


def apply_kernel(high_ref, low_ref, pair_in, partial_ref, *outputs):
    total = dot_split((high_ref[...], low_ref[...]), halves(pair_in[...])) + partial_ref[...]
    at = 0
    for ref in outputs:
        ref[...] = total[at : at + ref.shape[0]]
        at += ref.shape[0]


def last_kernel(high_ref, low_ref, pair_in, partial_ref, out_ref, result, sems):
    columns = pair_in.shape[1]
    chunk = columns // sems.shape[0]
    copies = []
    for number in range(sems.shape[0]):
        at = pl.ds(number * chunk, chunk)
        result[:, at] = dot_split((high_ref[...], low_ref[...]), halves(pair_in[:, at])) + partial_ref[:, at]
        copies.append(pltpu.make_async_copy(result.at[:, at], out_ref.at[:, at], sems.at[number]))
        copies[-1].start()
    for copy in copies:
        copy.wait()


def call(kernel, in_spaces, outs, scratch=(), out_space=pltpu.VMEM):
    return pl.pallas_call(
        kernel,
        in_specs=[pl.BlockSpec(memory_space=space) for space in in_spaces],
        out_specs=[pl.BlockSpec(memory_space=out_space) for _ in outs],
        out_shape=[jax.ShapeDtypeStruct(shape, dtype) for shape, dtype in outs],
        scratch_shapes=list(scratch),
        compiler_params=pltpu.CompilerParams(vmem_limit_bytes=VMEM_LIMIT),
    )


def on_device(eigvecs, panels, sweep_shift, slot_group):
    sweeps, _, panel_rows, band = panels.shape
    rows_dev, cols_dev = eigvecs.shape
    half = rows_dev // 2
    row_count, col_count = lax.axis_size("row"), lax.axis_size("col")
    piece = panel_rows // row_count
    smem, vmem = pltpu.SMEM, pltpu.VMEM
    place = jnp.stack([lax.axis_index("row") % 2, lax.axis_index("col")]).astype(jnp.int32)

    core_route = [(i, i ^ 1) for i in range(row_count)]
    pair_route = [(i, (i + 1 if i % 2 else i - 1) % row_count) for i in range(row_count)]

    split = panels.reshape(sweeps, row_count, piece, band).transpose(1, 0, 2, 3)
    pieces = lax.all_to_all(split, "row", 0, 0, tiled=True)
    columns = tuple(range(col_count))
    paired = col_count == 2
    if paired:
        one, two = (0,), (1,)
        layout = (
            ((0, columns, 0),),
            ((1, one, 0), (1, two, 1)),
            ((2, one, 0),),
            ((3, one, 0), (3, two, 1)),
            ((2, two, 0),),
        )
        groups = ((1, 2), (3,))
    else:
        layout = (
            ((0, columns, 0),),
            ((1, columns, 0), (2, columns, 1)),
            ((3, columns, 0),),
            ((4, columns, 0), (5, columns, 1)),
            ((6, columns, 0),),
        )
        groups = ()
    blocks = 1 + max(target[0] for targets in layout for target in targets)
    shape = (row_count, col_count, blocks, piece, band)
    (routed,) = call(
        functools.partial(reorder_kernel, layout),
        (smem, smem, vmem),
        [(shape, F32)],
        [vmem(shape, F32), pltpu.SemaphoreType.DMA(())],
        pltpu.HBM,
    )(sweep_shift, slot_group, pieces)
    flat = routed.reshape((row_count * col_count, blocks, piece, band))
    recv = lax.all_to_all(flat, ("row", "col"), 0, 0, tiled=True).reshape(shape)

    block = ((half, cols_dev), F32)
    whole = ((rows_dev, cols_dev), F32)
    handed = [((row_count, col_count, len(group), piece, band), F32) for group in groups]
    scratch = [vmem((rows_dev, band), F32), pltpu.SemaphoreType.DMA((3,))]
    kernel = functools.partial(first_kernel, groups)
    for_core, for_pair, *here = call(kernel, (smem, vmem, vmem), [block, block, *handed], scratch)(place, recv, eigvecs)

    def operators(number, for_exchange, from_core, for_core, for_pair):
        if paired:
            sources = (here[0], there[0]) if number == 0 else (here[0], there[0], here[1], there[1])
            if number == 0:
                odd, even = (((0, 0), (1, 0)), ((1, 0), (0, 0))), ((0, 1), (1, 1))
            else:
                odd, even = (((2, 0), (3, 0)), ((3, 0), (2, 0))), ((1, 1), (0, 1))
        else:
            sources = (recv,)
            odd, even = (((0, 1 + 3 * number),), ((0, 2 + 3 * number),)), ((0, 3 + 3 * number),)
        kernel = functools.partial(operator_kernel, odd, even, for_exchange)
        weight = ((rows_dev, half), BF16)
        inputs = (place, *sources, from_core, for_core, for_pair)
        return call(kernel, (smem,) + (vmem,) * (len(inputs) - 1), [whole, weight, weight])(*inputs)

    from_pair = lax.ppermute(for_pair, "row", pair_route)
    from_core = lax.ppermute(for_core, "row", core_route)
    there = [lax.ppermute(tiles, "col", [(0, 1), (1, 0)]) for tiles in here]
    partial, high, low = operators(0, True, from_core, for_core, for_pair)
    for_core, for_pair = call(apply_kernel, (vmem,) * 4, [block] * 2)(high, low, from_pair, partial)
    from_pair = lax.ppermute(for_pair, "row", pair_route)
    from_core = lax.ppermute(for_core, "row", core_route)
    partial, high, low = operators(1, False, from_core, for_core, for_pair)
    chunks = [vmem(*whole), pltpu.SemaphoreType.DMA((4 if cols_dev % 512 == 0 else 1,))]
    return call(last_kernel, (vmem,) * 4, [whole], chunks, pl.ANY)(high, low, from_pair, partial)[0]


def solution(mesh):
    in_specs = (P("row", "col"), P(None, "row", "col", None), P(), P())
    return jax.shard_map(on_device, mesh=mesh, in_specs=in_specs, out_specs=P("row", "col"), check_vma=False)
```

time: 83.7 us -> 74.3 us (0.89)
  waiting for transfers between devices: 40.6 us -> 30.7 us
    all_to_all x1, waiting for transfers between devices: 23.4 us -> 15.7 us  [on_device(): recv = lax.all_to_all(flat, ('row', 'col'), 0, 0, tiled=True).reshape(shape)]
    ppermute x4 -> x6, waiting for transfers between devices: 17.2 us -> 15 us  [the longest x2 9.79 us: on_device(): there = [lax.ppermute(tiles, 'col', [(0, 1), (1, 0)]) for tiles in here]]
    ppermute x4 -> x6, starting transfers between devices: 3.43 us -> 4.13 us  [the longest x2 2.22 us: on_device(): from_pair = lax.ppermute(for_pair, 'row', pair_route)]
    pallas_call x5 -> x6, Pallas kernels: 17.1 us -> 16.7 us  [the longest x2 10 us: operators(): call(kernel, (smem,) + (vmem,) * (len(inputs) - 1), [whole, weight, weight])]
  transfers between devices with their start and end apart: 5 -> 7, of which waited for: 4 -> 5; matrix products, arithmetic and copies ran while one was open for 0% -> 0% of each run, Pallas kernels for 10% -> 14%
where the time goes in v1:
time: 74.3 us; the launch traced here: 74 us
  waiting for transfers between devices  30.7 us (41%)
  blocking collectives  17.9 us (24%)
  Pallas kernels  16.7 us (22%)
  starting transfers between devices  7.46 us (10%)
  local copies, waits for them, and re-layouts  1.01 us (1%)
    all_to_all x1, blocking collectives, on_device(): pieces = lax.all_to_all(split, 'row', 0, 0, tiled=True)  17.9 us
    all_to_all x1, waiting for transfers between devices, on_device(): recv = lax.all_to_all(flat, ('row', 'col'), 0, 0, tiled=True).reshape(shape)  15.7 us
    pallas_call x2, Pallas kernels, operators(): call(kernel, (smem,) + (vmem,) * (len(inputs) - 1), [whole, weight, weight])  10 us
    ppermute x2, waiting for transfers between devices, on_device(): there = [lax.ppermute(tiles, 'col', [(0, 1), (1, 0)]) for tiles in here]  9.79 us
    ppermute x2, waiting for transfers between devices, on_device(): from_pair = lax.ppermute(for_pair, 'row', pair_route)  5.22 us
    all_to_all x1, starting transfers between devices, on_device(): recv = lax.all_to_all(flat, ('row', 'col'), 0, 0, tiled=True).reshape(shape)  3.33 us
    pallas_call x1, Pallas kernels, on_device(): call(kernel, (smem, vmem, vmem), [block, block, *handed], scratch)  3.3 us
    ppermute x2, starting transfers between devices, on_device(): from_pair = lax.ppermute(for_pair, 'row', pair_route)  2.22 us
  transfers between devices with their start and end apart: 7, of which 5 were waited for; matrix products, arithmetic and copies ran while one was open for 0% of the time, Pallas kernels for 14%

profile of v1, /device:TPU:1, one launch (start us, length us, event | category | flops | bytes accessed | tf_op | source)
XLA Modules:
  0.0 74.0 jit_solution(4483274917033220695)
XLA Ops:
  0.0 0.0 copy-start
  0.0 1.0 %copy-done = f32[5,1,128,128]{3,2,1,0:T(8,128)S(1)} copy-done((f32[5,1,128,128]{3,2,1,0:T(8,128)S(1)}, f32[5,1,128,128]{3,2,1,0:T(8,128)}, u32[]{:S(2)}) %copy-start) | copy-done | bytes 327704
  1.0 0.0 copy-start.2
  1.0 0.0 copy-start.3
  1.0 17.9 %all_to_all.10.pieces_ref = f32[16,5,8,128]{3,2,1,0:T(8,128)S(1)} all-to-all(f32[16,5,8,128]{3,2,1,0:T(8,128)S(1)} %copy_bitcast_fusion), channel_id=1, replica_groups=mesh['row'=16,'col'=2] {'row'}, dimensions={0} | all-to-all | bytes 655360 | tf_op jit(solution)/shard_map/all_to_all | solution.py:236
  18.9 0.0 copy-done.2
  18.9 0.0 copy-done.3
  18.9 0.0 copy-start.1
  18.9 1.6 %shard_map.46 = f32[16,2,4,8,128]{4,3,2,1,0:T(8,128)} custom-call(s32[5]{0:T(128)S(1)} %copy-done.3, s32[5,16]{1,0:T(8,128)S(1)} %copy-done.2, f32[16,5,8,128]{3,2,1,0:T(8,128)S(1)} %all_to_all.10.pieces_ref), custom_call_target="tpu_custom_call" | custom-call | tf_op jit(solution)/shard_map/pallas_call | solution.py:260
  20.6 3.3 %all-to-all-start.1 = ((f32[32,4,8,128]{3,2,1,0:T(8,128)}), f32[32,4,8,128]{3,2,1,0:T(8,128)S(1)}, u32[]{:S(2)}, u32[]{:S(2)}) async-start(f32[32,4,8,128]{3,2,1,0:T(8,128)} %bitcast.4), calls=%async_computation.1 | async-start | bytes 1048576 | tf_op jit(solution)/shard_map/all_to_all | solution.py:268
  23.9 0.1 pad_add_fusion.place_ref
  24.0 15.7 %all-to-all-done.1 = f32[32,4,8,128]{3,2,1,0:T(8,128)S(1)} async-done(((f32[32,4,8,128]{3,2,1,0:T(8,128)}), f32[32,4,8,128]{3,2,1,0:T(8,128)S(1)}, u32[]{:S(2)}, u32[]{:S(2)}) %all-to-all-start.1) | async-done | bytes 524320 | tf_op jit(solution)/shard_map/all_to_all | solution.py:268
  39.7 0.0 copy-done.1
  39.7 3.3 %shard_map.47 = (f32[128,1024]{1,0:T(8,128)S(1)}, f32[128,1024]{1,0:T(8,128)S(1)}, f32[16,2,2,8,128]{4,3,2,1,0:T(8,128)S(1)}, f32[16,2,1,8,128]{4,3,2,1,0:T(8,128)S(1)}) custom-call(s32[2]{0:T(128)S(1)} %pad_add_fusion.place_ref, f32[16,2,4,8,128]{4,3,2,1,0:T(8,128)S(1)} %bitcast.9, f32[256,1024]{1,0:T(8,128)S(1)} %copy-done.1), custom_call_target="tpu_custom_call" | custom-call | tf_op jit(solution)/shard_map/pallas_call | solution.py:275
  43.0 0.1 collective-permute-start.2
  43.1 1.1 %collective-permute-start.3 = (f32[128,1024]{1,0:T(8,128)S(1)}, f32[128,1024]{1,0:T(8,128)S(1)}, u32[]{:S(2)}, u32[]{:S(2)}) collective-permute-start(f32[128,1024]{1,0:T(8,128)S(1)} %get-tuple-element.20.refs_4_), channel_id=1, source_target_pairs={{0,30},{2,4},{4,2},{6,8},{8,6},{10,12},{12,10},{14,16},{16,14},{18... | collective-permute-start | bytes 1572872 | tf_op jit(solution)/shard_map/ppermute | solution.py:292
  44.2 0.7 collective-permute-start
  44.9 6.1 %collective-permute-done.refs_1_ = f32[16,2,2,8,128]{4,3,2,1,0:T(8,128)S(1)} collective-permute-done((f32[16,2,2,8,128]{4,3,2,1,0:T(8,128)S(1)}, f32[16,2,2,8,128]{4,3,2,1,0:T(8,128)S(1)}, u32[]{:S(2)}, u32[]{:S(2)}) %collective-permute-start) | collective-permute-done | bytes 262176 | tf_op jit(solution)/shard_map/ppermute | solution.py:294
  51.0 0.0 collective-permute-done.2.refs_2_
  51.0 5.0 %shard_map.48 = (f32[256,1024]{1,0:T(8,128)S(1)}, bf16[256,128]{1,0:T(8,128)(2,1)S(1)}, bf16[256,128]{1,0:T(8,128)(2,1)S(1)}) custom-call(s32[2]{0:T(128)S(1)} %pad_add_fusion.place_ref, f32[16,2,2,8,128]{4,3,2,1,0:T(8,128)S(1)} %get-tuple-element.17.refs_0_, f32[16,2,2,8,128]{4,3,2,1,0:T(8,128)S(1)} %collective-permute-done.refs_1_, ...), custom_call_target="tpu_custom_call" | custom-call | tf_op jit(solution)/shard_map/pallas_call | solution.py:290
  56.0 1.4 %collective-permute-done.3.pair_in = f32[128,1024]{1,0:T(8,128)S(1)} collective-permute-done((f32[128,1024]{1,0:T(8,128)S(1)}, f32[128,1024]{1,0:T(8,128)S(1)}, u32[]{:S(2)}, u32[]{:S(2)}) %collective-permute-start.3) | collective-permute-done | bytes 524320 | tf_op jit(solution)/shard_map/ppermute | solution.py:292
  57.4 0.5 shard_map.49
  57.9 0.6 collective-permute-start.4
  58.5 1.2 %collective-permute-start.5 = (f32[128,1024]{1,0:T(8,128)S(1)}, f32[128,1024]{1,0:T(8,128)S(1)}, u32[]{:S(2)}, u32[]{:S(2)}) collective-permute-start(f32[128,1024]{1,0:T(8,128)S(1)} %get-tuple-element.25.refs_6_), channel_id=1, source_target_pairs={{0,30},{2,4},{4,2},{6,8},{8,6},{10,12},{12,10},{14,16},{16,14},{18... | collective-permute-start | bytes 1572872 | tf_op jit(solution)/shard_map/ppermute | solution.py:297
  59.6 0.5 collective-permute-start.1
  60.1 3.7 %collective-permute-done.1.refs_3_ = f32[16,2,1,8,128]{4,3,2,1,0:T(8,128)S(1)} collective-permute-done((f32[16,2,1,8,128]{4,3,2,1,0:T(8,128)S(1)}, f32[16,2,1,8,128]{4,3,2,1,0:T(8,128)S(1)}, u32[]{:S(2)}, u32[]{:S(2)}) %collective-permute-start.1) | collective-permute-done | bytes 131104 | tf_op jit(solution)/shard_map/ppermute | solution.py:294
  63.8 0.0 collective-permute-done.4.refs_4_
  63.8 5.0 %shard_map.50 = (f32[256,1024]{1,0:T(8,128)S(1)}, bf16[256,128]{1,0:T(8,128)(2,1)S(1)}, bf16[256,128]{1,0:T(8,128)(2,1)S(1)}) custom-call(s32[2]{0:T(128)S(1)} %pad_add_fusion.place_ref, f32[16,2,2,8,128]{4,3,2,1,0:T(8,128)S(1)} %get-tuple-element.17.refs_0_, f32[16,2,2,8,128]{4,3,2,1,0:T(8,128)S(1)} %collective-permute-done.refs_1_, ...), custom_call_target="tpu_custom_call" | custom-call | tf_op jit(solution)/shard_map/pallas_call | solution.py:290
  68.8 3.9 %collective-permute-done.5.pair_in = f32[128,1024]{1,0:T(8,128)S(1)} collective-permute-done((f32[128,1024]{1,0:T(8,128)S(1)}, f32[128,1024]{1,0:T(8,128)S(1)}, u32[]{:S(2)}, u32[]{:S(2)}) %collective-permute-start.5) | collective-permute-done | bytes 524320 | tf_op jit(solution)/shard_map/ppermute | solution.py:297
  72.7 1.3 %shard_map.51 = f32[256,1024]{1,0:T(8,128)} custom-call(bf16[256,128]{1,0:T(8,128)(2,1)S(1)} %get-tuple-element.26.high_ref, bf16[256,128]{1,0:T(8,128)(2,1)S(1)} %get-tuple-element.27.low_ref, f32[128,1024]{1,0:T(8,128)S(1)} %collective-permute-done.5.pair_in, f32[256,1024]{1,0:T(8,128)S(1)} %get-tuple-element.28.partial_ref), custom_call_target="tpu_custom_call" | custom-call | tf_op jit(solution)/shard_map/pallas_call | solution.py:301
  (1 shorter events, 0.0 us)
Async XLA Ops:
  0.0 1.0 %copy-start = (f32[5,1,128,128]{3,2,1,0:T(8,128)S(1)}, f32[5,1,128,128]{3,2,1,0:T(8,128)}, u32[]{:S(2)}) copy-start(f32[5,1,128,128]{3,2,1,0:T(8,128)} %param.5) | copy-start | bytes 983044
  1.0 17.9 %copy-start.2 = (s32[5,16]{1,0:T(8,128)S(1)}, s32[5,16]{1,0:T(8,128)}, u32[]{:S(2)}) copy-start(s32[5,16]{1,0:T(8,128)} %group_ref.1) | copy-start | bytes 964
  1.0 17.9 %copy-start.3 = (s32[5]{0:T(128)S(1)}, s32[5]{0:T(128)}, u32[]{:S(2)}) copy-start(s32[5]{0:T(128)} %shift_ref.1) | copy-start | bytes 64
  18.9 20.8 %copy-start.1 = (f32[256,1024]{1,0:T(8,128)S(1)}, f32[256,1024]{1,0:T(8,128)}, u32[]{:S(2)}) copy-start(f32[256,1024]{1,0:T(8,128)} %z_ref.1) | copy-start | bytes 3145732
  20.6 19.2 %all-to-all-start.1 = ((f32[32,4,8,128]{3,2,1,0:T(8,128)}), f32[32,4,8,128]{3,2,1,0:T(8,128)S(1)}, u32[]{:S(2)}, u32[]{:S(2)}) async-start(f32[32,4,8,128]{3,2,1,0:T(8,128)} %bitcast.4), calls=%async_computation.1 | async-start | bytes 1048576 | tf_op jit(solution)/shard_map/all_to_all | solution.py:268
  43.0 8.0 %collective-permute-start.2 = (f32[128,1024]{1,0:T(8,128)S(1)}, f32[128,1024]{1,0:T(8,128)S(1)}, u32[]{:S(2)}, u32[]{:S(2)}) collective-permute-start(f32[128,1024]{1,0:T(8,128)S(1)} %get-tuple-element.19.refs_3_), channel_id=1, source_target_pairs={{0,2},{2,0},{4,6},{6,4},{8,10},{10,8},{12,14},{14,12},{16,18},{18,... | collective-permute-start | bytes 1572872 | tf_op jit(solution)/shard_map/ppermute | solution.py:293
  43.1 14.3 %collective-permute-start.3 = (f32[128,1024]{1,0:T(8,128)S(1)}, f32[128,1024]{1,0:T(8,128)S(1)}, u32[]{:S(2)}, u32[]{:S(2)}) collective-permute-start(f32[128,1024]{1,0:T(8,128)S(1)} %get-tuple-element.20.refs_4_), channel_id=1, source_target_pairs={{0,30},{2,4},{4,2},{6,8},{8,6},{10,12},{12,10},{14,16},{16,14},{18... | collective-permute-start | bytes 1572872 | tf_op jit(solution)/shard_map/ppermute | solution.py:292
  44.2 6.8 %collective-permute-start = (f32[16,2,2,8,128]{4,3,2,1,0:T(8,128)S(1)}, f32[16,2,2,8,128]{4,3,2,1,0:T(8,128)S(1)}, u32[]{:S(2)}, u32[]{:S(2)}) collective-permute-start(f32[16,2,2,8,128]{4,3,2,1,0:T(8,128)S(1)} %get-tuple-element.17.refs_0_), channel_id=1, source_target_pairs={{0,1},{1,0},{2,3},{3,2},{4,5},{5,4},{6,7},{7,6},{8,9},{9,8},{10,11... | collective-permute-start | bytes 786440 | tf_op jit(solution)/shard_map/ppermute | solution.py:294
  57.9 6.0 %collective-permute-start.4 = (f32[128,1024]{1,0:T(8,128)S(1)}, f32[128,1024]{1,0:T(8,128)S(1)}, u32[]{:S(2)}, u32[]{:S(2)}) collective-permute-start(f32[128,1024]{1,0:T(8,128)S(1)} %get-tuple-element.24.refs_5_), channel_id=1, source_target_pairs={{0,2},{2,0},{4,6},{6,4},{8,10},{10,8},{12,14},{14,12},{16,18},{18,... | collective-permute-start | bytes 1572872 | tf_op jit(solution)/shard_map/ppermute | solution.py:298
  58.5 14.2 %collective-permute-start.5 = (f32[128,1024]{1,0:T(8,128)S(1)}, f32[128,1024]{1,0:T(8,128)S(1)}, u32[]{:S(2)}, u32[]{:S(2)}) collective-permute-start(f32[128,1024]{1,0:T(8,128)S(1)} %get-tuple-element.25.refs_6_), channel_id=1, source_target_pairs={{0,30},{2,4},{4,2},{6,8},{8,6},{10,12},{12,10},{14,16},{16,14},{18... | collective-permute-start | bytes 1572872 | tf_op jit(solution)/shard_map/ppermute | solution.py:297
  59.6 4.2 %collective-permute-start.1 = (f32[16,2,1,8,128]{4,3,2,1,0:T(8,128)S(1)}, f32[16,2,1,8,128]{4,3,2,1,0:T(8,128)S(1)}, u32[]{:S(2)}, u32[]{:S(2)}) collective-permute-start(f32[16,2,1,8,128]{4,3,2,1,0:T(8,128)S(1)} %get-tuple-element.18.refs_2_), channel_id=1, source_target_pairs={{0,1},{1,0},{2,3},{3,2},{4,5},{5,4},{6,7},{7,6},{8,9},{9,8},{10,11... | collective-permute-start | bytes 393224 | tf_op jit(solution)/shard_map/ppermute | solution.py:294

commit v2 on v1

--- a/solution.py
+++ b/solution.py
@@ -100,7 +100,7 @@
     return jnp.where(index >= size, index - size, index)
 
 
-def reorder_kernel(layout, shift_ref, group_ref, pieces_ref, out_ref, buffer, sem):
+def reorder_kernel(layout, shift_ref, group_ref, pieces_ref, out_ref):
     slots = pieces_ref.shape[0]
     for slot in range(slots):
         for sweep, targets in enumerate(layout):
@@ -109,10 +109,7 @@
             for block, columns, distance in targets:
                 target = wrapped(window + 1, slots) if distance else window
                 for c in columns:
-                    buffer[target, c, block] = piece
-    copy = pltpu.make_async_copy(buffer, out_ref, sem)
-    copy.start()
-    copy.wait()
+                    out_ref[target, c, block] = piece
 
 
 def fetch_panel(recv_ref, *index):
@@ -155,7 +152,7 @@
 
 
 def operator_kernel(odd, even, for_exchange, place_ref, *refs):
-    sources, (core_in, core_own, pair_own, partial_ref, high_ref, low_ref) = refs[:-6], refs[-6:]
+    sources, (core_own, pair_own, partial_ref, high_ref, low_ref) = refs[:-5], refs[-5:]
     parity, column = place_ref[0], place_ref[1]
 
     def panel_of(choices):
@@ -182,27 +179,27 @@
     left = dot_split(halves(last[:, :half]), halves(other))
     right = dot_split(halves(last[:, half:]), halves(own))
     natural = (left[:, :half], left[:, half:], right[:, :half], right[:, half:])
-    first, *rest = arranged(parity, natural)
-    high_ref[...], low_ref[...] = halves(first)
-    rows = jnp.concatenate([core_in[...], core_own[...], pair_own[...]], axis=0)
-    partial_ref[...] = dot_split(halves(jnp.concatenate(rest, axis=1)), halves(rows))
-
-
-def apply_kernel(high_ref, low_ref, pair_in, partial_ref, *outputs):
-    total = dot_split((high_ref[...], low_ref[...]), halves(pair_in[...])) + partial_ref[...]
+    pair_columns, core_columns, *rest = arranged(parity, natural)
+    high_ref[...], low_ref[...] = halves(beside(pair_columns, core_columns))
+    partial_ref[...] = dot_split(halves(beside(*rest)), halves(above(core_own[...], pair_own[...])))
+
+
+def apply_kernel(high_ref, low_ref, pair_in, core_in, partial_ref, *outputs):
+    total = dot_split((high_ref[...], low_ref[...]), halves(above(pair_in[...], core_in[...]))) + partial_ref[...]
     at = 0
     for ref in outputs:
         ref[...] = total[at : at + ref.shape[0]]
         at += ref.shape[0]
 
 
-def last_kernel(high_ref, low_ref, pair_in, partial_ref, out_ref, result, sems):
+def last_kernel(high_ref, low_ref, pair_in, core_in, partial_ref, out_ref, result, sems):
     columns = pair_in.shape[1]
     chunk = columns // sems.shape[0]
     copies = []
     for number in range(sems.shape[0]):
         at = pl.ds(number * chunk, chunk)
-        result[:, at] = dot_split((high_ref[...], low_ref[...]), halves(pair_in[:, at])) + partial_ref[:, at]
+        far = halves(above(pair_in[:, at], core_in[:, at]))
+        result[:, at] = dot_split((high_ref[...], low_ref[...]), far) + partial_ref[:, at]
         copies.append(pltpu.make_async_copy(result.at[:, at], out_ref.at[:, at], sems.at[number]))
         copies[-1].start()
     for copy in copies:
@@ -232,6 +229,7 @@
     core_route = [(i, i ^ 1) for i in range(row_count)]
     pair_route = [(i, (i + 1 if i % 2 else i - 1) % row_count) for i in range(row_count)]
 
+    panels, place = lax.optimization_barrier((panels, place))
     split = panels.reshape(sweeps, row_count, piece, band).transpose(1, 0, 2, 3)
     pieces = lax.all_to_all(split, "row", 0, 0, tiled=True)
     columns = tuple(range(col_count))
@@ -261,8 +259,6 @@
         functools.partial(reorder_kernel, layout),
         (smem, smem, vmem),
         [(shape, F32)],
-        [vmem(shape, F32), pltpu.SemaphoreType.DMA(())],
-        pltpu.HBM,
     )(sweep_shift, slot_group, pieces)
     flat = routed.reshape((row_count * col_count, blocks, piece, band))
     recv = lax.all_to_all(flat, ("row", "col"), 0, 0, tiled=True).reshape(shape)
@@ -274,7 +270,7 @@
     kernel = functools.partial(first_kernel, groups)
     for_core, for_pair, *here = call(kernel, (smem, vmem, vmem), [block, block, *handed], scratch)(place, recv, eigvecs)
 
-    def operators(number, for_exchange, from_core, for_core, for_pair):
+    def operators(number, for_exchange, for_core, for_pair):
         if paired:
             sources = (here[0], there[0]) if number == 0 else (here[0], there[0], here[1], there[1])
             if number == 0:
@@ -285,20 +281,25 @@
             sources = (recv,)
             odd, even = (((0, 1 + 3 * number),), ((0, 2 + 3 * number),)), ((0, 3 + 3 * number),)
         kernel = functools.partial(operator_kernel, odd, even, for_exchange)
-        weight = ((rows_dev, half), BF16)
-        inputs = (place, *sources, from_core, for_core, for_pair)
+        weight = ((rows_dev, rows_dev), BF16)
+        inputs = (place, *sources, for_core, for_pair)
         return call(kernel, (smem,) + (vmem,) * (len(inputs) - 1), [whole, weight, weight])(*inputs)
 
-    from_pair = lax.ppermute(for_pair, "row", pair_route)
-    from_core = lax.ppermute(for_core, "row", core_route)
-    there = [lax.ppermute(tiles, "col", [(0, 1), (1, 0)]) for tiles in here]
-    partial, high, low = operators(0, True, from_core, for_core, for_pair)
-    for_core, for_pair = call(apply_kernel, (vmem,) * 4, [block] * 2)(high, low, from_pair, partial)
-    from_pair = lax.ppermute(for_pair, "row", pair_route)
-    from_core = lax.ppermute(for_core, "row", core_route)
-    partial, high, low = operators(1, False, from_core, for_core, for_pair)
+    def exchange(number, for_core, for_pair):
+        from_pair = lax.ppermute(for_pair, "row", pair_route)
+        if paired:
+            there.append(lax.ppermute(here[number], "col", [(0, 1), (1, 0)]))
+            for_core, there[number] = lax.optimization_barrier((for_core, there[number]))
+        return from_pair, lax.ppermute(for_core, "row", core_route)
+
+    there = []
+    received = exchange(0, for_core, for_pair)
+    partial, high, low = operators(0, True, for_core, for_pair)
+    for_core, for_pair = call(apply_kernel, (vmem,) * 5, [block] * 2)(high, low, *received, partial)
+    received = exchange(1, for_core, for_pair)
+    partial, high, low = operators(1, False, for_core, for_pair)
     chunks = [vmem(*whole), pltpu.SemaphoreType.DMA((4 if cols_dev % 512 == 0 else 1,))]
-    return call(last_kernel, (vmem,) * 4, [whole], chunks, pl.ANY)(high, low, from_pair, partial)[0]
+    return call(last_kernel, (vmem,) * 5, [whole], chunks, pl.ANY)(high, low, *received, partial)[0]
 
 
 def solution(mesh):

time: 74.3 us -> 73.2 us (0.985)
  blocking collectives: 17.9 us -> 36.9 us
  waiting for transfers between devices: 30.7 us -> 15.1 us
  starting transfers between devices: 7.46 us -> 4.37 us
  Pallas kernels: 16.7 us -> 15.5 us
    all_to_all x0 -> x1, blocking collectives: none -> 18.9 us  [on_device(): recv = lax.all_to_all(flat, ('row', 'col'), 0, 0, tiled=True).reshape(shape)]
    all_to_all x1 -> x0, waiting for transfers between devices: 15.7 us -> none  [on_device(): recv = lax.all_to_all(flat, ('row', 'col'), 0, 0, tiled=True).reshape(shape)]
    all_to_all x1 -> x0, starting transfers between devices: 3.33 us -> none  [on_device(): recv = lax.all_to_all(flat, ('row', 'col'), 0, 0, tiled=True).reshape(shape)]
    pallas_call x1, Pallas kernels: 1.61 us -> 0.81 us  [on_device(): call(functools.partial(reorder_kernel, layout), (smem, smem, vmem), [(sha...]
  transfers between devices with their start and end apart: 7 -> 6, of which waited for: 5 -> 3; matrix products, arithmetic and copies ran while one was open for 0% -> 0% of each run, Pallas kernels for 14% -> 14%
where the time goes in v2:
time: 73.2 us; the launch traced here: 73 us
  blocking collectives  36.9 us (50%)
  Pallas kernels  15.5 us (21%)
  waiting for transfers between devices  15.1 us (21%)
  starting transfers between devices  4.37 us (6%)
  local copies, waits for them, and re-layouts  0.94 us (1%)
    all_to_all x1, blocking collectives, on_device(): recv = lax.all_to_all(flat, ('row', 'col'), 0, 0, tiled=True).reshape(shape)  18.9 us
    all_to_all x1, blocking collectives, on_device(): pieces = lax.all_to_all(split, 'row', 0, 0, tiled=True)  17.9 us
    pallas_call x2, Pallas kernels, operators(): call(kernel, (smem,) + (vmem,) * (len(inputs) - 1), [whole, weight, weight])  9.33 us
    ppermute x2, waiting for transfers between devices, exchange(): from_pair = lax.ppermute(for_pair, 'row', pair_route)  8.9 us
    ppermute x2, waiting for transfers between devices, exchange(): there.append(lax.ppermute(here[number], 'col', [(0, 1), (1, 0)]))  6.23 us
    ppermute x2, starting transfers between devices, exchange(): from_pair = lax.ppermute(for_pair, 'row', pair_route)  3.8 us
    pallas_call x1, Pallas kernels, on_device(): call(kernel, (smem, vmem, vmem), [block, block, *handed], scratch)  3.36 us
  transfers between devices with their start and end apart: 6, of which 3 were waited for; matrix products, arithmetic and copies ran while one was open for 0% of the time, Pallas kernels for 14%

profile of v2, /device:TPU:1, one launch (start us, length us, event | category | flops | bytes accessed | tf_op | source)
XLA Modules:
  0.0 73.0 jit_solution(9314217181137903870)
XLA Ops:
  0.0 0.0 copy-start
  0.0 0.1 pad_add_fusion.place_ref
  0.1 0.9 %copy-done = f32[5,1,128,128]{3,2,1,0:T(8,128)S(1)} copy-done((f32[5,1,128,128]{3,2,1,0:T(8,128)S(1)}, f32[5,1,128,128]{3,2,1,0:T(8,128)}, u32[]{:S(2)}) %copy-start) | copy-done | bytes 327704
  1.0 0.0 copy-start.2
  1.0 0.0 copy-start.3
  1.0 17.9 %all_to_all.10.pieces_ref = f32[16,5,8,128]{3,2,1,0:T(8,128)S(1)} all-to-all(f32[16,5,8,128]{3,2,1,0:T(8,128)S(1)} %copy_bitcast_fusion), channel_id=1, replica_groups=mesh['row'=16,'col'=2] {'row'}, dimensions={0} | all-to-all | bytes 655360 | tf_op jit(solution)/shard_map/all_to_all | solution.py:234
  18.9 0.0 copy-done.2
  18.9 0.0 copy-done.3
  18.9 0.0 copy-start.1
  18.9 0.8 %shard_map.46 = f32[16,2,4,8,128]{4,3,2,1,0:T(8,128)S(1)} custom-call(s32[5]{0:T(128)S(1)} %copy-done.3, s32[5,16]{1,0:T(8,128)S(1)} %copy-done.2, f32[16,5,8,128]{3,2,1,0:T(8,128)S(1)} %all_to_all.10.pieces_ref), custom_call_target="tpu_custom_call" | custom-call | tf_op jit(solution)/shard_map/pallas_call | solution.py:258
  19.8 18.9 %all_to_all.11 = f32[32,4,8,128]{3,2,1,0:T(8,128)S(1)} all-to-all(f32[32,4,8,128]{3,2,1,0:T(8,128)S(1)} %bitcast.10), channel_id=1, replica_groups=mesh['row'=16,'col'=2] {'row','col'}, dimensions={0} | all-to-all | bytes 1048576 | tf_op jit(solution)/shard_map/all_to_all | solution.py:264
  38.7 0.0 copy-done.1
  38.7 3.4 %shard_map.47 = (f32[128,1024]{1,0:T(8,128)S(1)}, f32[128,1024]{1,0:T(8,128)S(1)}, f32[16,2,2,8,128]{4,3,2,1,0:T(8,128)S(1)}, f32[16,2,1,8,128]{4,3,2,1,0:T(8,128)S(1)}) custom-call(s32[2]{0:T(128)S(1)} %pad_add_fusion.place_ref, f32[16,2,4,8,128]{4,3,2,1,0:T(8,128)S(1)} %bitcast.9, f32[256,1024]{1,0:T(8,128)S(1)} %copy-done.1), custom_call_target="tpu_custom_call" | custom-call | tf_op jit(solution)/shard_map/pallas_call | solution.py:271
  42.1 0.1 collective-permute-start
  42.2 2.0 %collective-permute-start.1 = (f32[128,1024]{1,0:T(8,128)S(1)}, f32[128,1024]{1,0:T(8,128)S(1)}, u32[]{:S(2)}, u32[]{:S(2)}) collective-permute-start(f32[128,1024]{1,0:T(8,128)S(1)} %get-tuple-element.29.refs_3_), channel_id=1, source_target_pairs={{0,30},{2,4},{4,2},{6,8},{8,6},{10,12},{12,10},{14,16},{16,14},{18... | collective-permute-start | bytes 1572872 | tf_op jit(solution)/shard_map/ppermute | solution.py:289
  44.1 6.2 %collective-permute-done.refs_1_ = f32[16,2,2,8,128]{4,3,2,1,0:T(8,128)S(1)} collective-permute-done((f32[16,2,2,8,128]{4,3,2,1,0:T(8,128)S(1)}, f32[16,2,2,8,128]{4,3,2,1,0:T(8,128)S(1)}, u32[]{:S(2)}, u32[]{:S(2)}) %collective-permute-start) | collective-permute-done | bytes 262176 | tf_op jit(solution)/shard_map/ppermute | solution.py:291
  50.4 0.3 collective-permute-start.2
  50.7 0.2 collective-permute-start.3
  50.9 4.7 %shard_map.48 = (f32[256,1024]{1,0:T(8,128)S(1)}, bf16[256,256]{1,0:T(8,128)(2,1)S(1)}, bf16[256,256]{1,0:T(8,128)(2,1)S(1)}) custom-call(s32[2]{0:T(128)S(1)} %pad_add_fusion.place_ref, f32[16,2,2,8,128]{4,3,2,1,0:T(8,128)S(1)} %get-tuple-element.25.refs_0_, f32[16,2,2,8,128]{4,3,2,1,0:T(8,128)S(1)} %collective-permute-done.refs_1_, ...), custom_call_target="tpu_custom_call" | custom-call | tf_op jit(solution)/shard_map/pallas_call | solution.py:286
  55.6 1.1 %collective-permute-done.1.pair_in = f32[128,1024]{1,0:T(8,128)S(1)} collective-permute-done((f32[128,1024]{1,0:T(8,128)S(1)}, f32[128,1024]{1,0:T(8,128)S(1)}, u32[]{:S(2)}, u32[]{:S(2)}) %collective-permute-start.1) | collective-permute-done | bytes 524320 | tf_op jit(solution)/shard_map/ppermute | solution.py:289
  56.6 0.0 collective-permute-done.2.core_in
  56.6 0.6 shard_map.49
  57.2 0.0 collective-permute-done.3.refs_3_
  57.3 1.8 %collective-permute-start.4 = (f32[128,1024]{1,0:T(8,128)S(1)}, f32[128,1024]{1,0:T(8,128)S(1)}, u32[]{:S(2)}, u32[]{:S(2)}) collective-permute-start(f32[128,1024]{1,0:T(8,128)S(1)} %get-tuple-element.36.refs_5_), channel_id=1, source_target_pairs={{0,30},{2,4},{4,2},{6,8},{8,6},{10,12},{12,10},{14,16},{16,14},{18... | collective-permute-start | bytes 1572872 | tf_op jit(solution)/shard_map/ppermute | solution.py:289
  59.1 0.0 collective-permute-start.5
  59.1 4.6 %shard_map.50 = (f32[256,1024]{1,0:T(8,128)S(1)}, bf16[256,256]{1,0:T(8,128)(2,1)S(1)}, bf16[256,256]{1,0:T(8,128)(2,1)S(1)}) custom-call(s32[2]{0:T(128)S(1)} %pad_add_fusion.place_ref, f32[16,2,2,8,128]{4,3,2,1,0:T(8,128)S(1)} %get-tuple-element.25.refs_0_, f32[16,2,2,8,128]{4,3,2,1,0:T(8,128)S(1)} %collective-permute-done.refs_1_, ...), custom_call_target="tpu_custom_call" | custom-call | tf_op jit(solution)/shard_map/pallas_call | solution.py:286
  63.7 7.8 %collective-permute-done.4.pair_in = f32[128,1024]{1,0:T(8,128)S(1)} collective-permute-done((f32[128,1024]{1,0:T(8,128)S(1)}, f32[128,1024]{1,0:T(8,128)S(1)}, u32[]{:S(2)}, u32[]{:S(2)}) %collective-permute-start.4) | collective-permute-done | bytes 524320 | tf_op jit(solution)/shard_map/ppermute | solution.py:289
  71.5 0.0 collective-permute-done.5.core_in
  71.5 1.4 %shard_map.51 = f32[256,1024]{1,0:T(8,128)} custom-call(bf16[256,256]{1,0:T(8,128)(2,1)S(1)} %get-tuple-element.37.high_ref, bf16[256,256]{1,0:T(8,128)(2,1)S(1)} %get-tuple-element.38.low_ref, f32[128,1024]{1,0:T(8,128)S(1)} %collective-permute-done.4.pair_in, f32[128,1024]{1,0:T(8,128)S(1)} %collective-permute-done.5.core_in, ...), custom_call_target="tpu_custom_call" | custom-call | tf_op jit(solution)/shard_map/pallas_call | solution.py:302
  (1 shorter events, 0.0 us)
Async XLA Ops:
  0.0 1.0 %copy-start = (f32[5,1,128,128]{3,2,1,0:T(8,128)S(1)}, f32[5,1,128,128]{3,2,1,0:T(8,128)}, u32[]{:S(2)}) copy-start(f32[5,1,128,128]{3,2,1,0:T(8,128)} %param.5) | copy-start | bytes 983044
  1.0 17.9 %copy-start.2 = (s32[5,16]{1,0:T(8,128)S(1)}, s32[5,16]{1,0:T(8,128)}, u32[]{:S(2)}) copy-start(s32[5,16]{1,0:T(8,128)} %group_ref.1) | copy-start | bytes 964
  1.0 17.9 %copy-start.3 = (s32[5]{0:T(128)S(1)}, s32[5]{0:T(128)}, u32[]{:S(2)}) copy-start(s32[5]{0:T(128)} %shift_ref.1) | copy-start | bytes 64
  18.9 19.8 %copy-start.1 = (f32[256,1024]{1,0:T(8,128)S(1)}, f32[256,1024]{1,0:T(8,128)}, u32[]{:S(2)}) copy-start(f32[256,1024]{1,0:T(8,128)} %z_ref.1) | copy-start | bytes 3145732
  42.1 8.3 %collective-permute-start = (f32[16,2,2,8,128]{4,3,2,1,0:T(8,128)S(1)}, f32[16,2,2,8,128]{4,3,2,1,0:T(8,128)S(1)}, u32[]{:S(2)}, u32[]{:S(2)}) collective-permute-start(f32[16,2,2,8,128]{4,3,2,1,0:T(8,128)S(1)} %get-tuple-element.25.refs_0_), channel_id=1, source_target_pairs={{0,1},{1,0},{2,3},{3,2},{4,5},{5,4},{6,7},{7,6},{8,9},{9,8},{10,11... | collective-permute-start | bytes 786440 | tf_op jit(solution)/shard_map/ppermute | solution.py:291
  42.2 14.5 %collective-permute-start.1 = (f32[128,1024]{1,0:T(8,128)S(1)}, f32[128,1024]{1,0:T(8,128)S(1)}, u32[]{:S(2)}, u32[]{:S(2)}) collective-permute-start(f32[128,1024]{1,0:T(8,128)S(1)} %get-tuple-element.29.refs_3_), channel_id=1, source_target_pairs={{0,30},{2,4},{4,2},{6,8},{8,6},{10,12},{12,10},{14,16},{16,14},{18... | collective-permute-start | bytes 1572872 | tf_op jit(solution)/shard_map/ppermute | solution.py:289
  50.4 6.3 %collective-permute-start.2 = (f32[128,1024]{1,0:T(8,128)S(1)}, f32[128,1024]{1,0:T(8,128)S(1)}, u32[]{:S(2)}, u32[]{:S(2)}) collective-permute-start(f32[128,1024]{1,0:T(8,128)S(1)} %get-tuple-element.32.refs_2_), channel_id=1, source_target_pairs={{0,2},{2,0},{4,6},{6,4},{8,10},{10,8},{12,14},{14,12},{16,18},{18,... | collective-permute-start | bytes 1572872 | tf_op jit(solution)/shard_map/ppermute | solution.py:293
  50.7 6.6 %collective-permute-start.3 = (f32[16,2,1,8,128]{4,3,2,1,0:T(8,128)S(1)}, f32[16,2,1,8,128]{4,3,2,1,0:T(8,128)S(1)}, u32[]{:S(2)}, u32[]{:S(2)}) collective-permute-start(f32[16,2,1,8,128]{4,3,2,1,0:T(8,128)S(1)} %get-tuple-element.28.refs_2_), channel_id=1, source_target_pairs={{0,1},{1,0},{2,3},{3,2},{4,5},{5,4},{6,7},{7,6},{8,9},{9,8},{10,11... | collective-permute-start | bytes 393224 | tf_op jit(solution)/shard_map/ppermute | solution.py:291
  57.3 14.3 %collective-permute-start.4 = (f32[128,1024]{1,0:T(8,128)S(1)}, f32[128,1024]{1,0:T(8,128)S(1)}, u32[]{:S(2)}, u32[]{:S(2)}) collective-permute-start(f32[128,1024]{1,0:T(8,128)S(1)} %get-tuple-element.36.refs_5_), channel_id=1, source_target_pairs={{0,30},{2,4},{4,2},{6,8},{8,6},{10,12},{12,10},{14,16},{16,14},{18... | collective-permute-start | bytes 1572872 | tf_op jit(solution)/shard_map/ppermute | solution.py:289
  59.1 12.5 %collective-permute-start.5 = (f32[128,1024]{1,0:T(8,128)S(1)}, f32[128,1024]{1,0:T(8,128)S(1)}, u32[]{:S(2)}, u32[]{:S(2)}) collective-permute-start(f32[128,1024]{1,0:T(8,128)S(1)} %get-tuple-element.39.refs_4_), channel_id=1, source_target_pairs={{0,2},{2,0},{4,6},{6,4},{8,10},{10,8},{12,14},{14,12},{16,18},{18,... | collective-permute-start | bytes 1572872 | tf_op jit(solution)/shard_map/ppermute | solution.py:293

commit v3 on v2

--- a/solution.py
+++ b/solution.py
@@ -10,6 +10,7 @@
 F32 = jnp.float32
 BF16 = jnp.bfloat16
 VMEM_LIMIT = 48 * 1024 * 1024
+OUT_CHUNKS = 2
 
 
 def mxu(a, b):
@@ -151,8 +152,9 @@
     ]
 
 
-def operator_kernel(odd, even, for_exchange, place_ref, *refs):
-    sources, (core_own, pair_own, partial_ref, high_ref, low_ref) = refs[:-5], refs[-5:]
+def operator_kernel(odd, even, for_exchange, known, place_ref, *refs):
+    partial_ref, high_ref, low_ref = refs[-3:]
+    sources, inputs = refs[: -3 - known], refs[-3 - known : -3]
     parity, column = place_ref[0], place_ref[1]
 
     def panel_of(choices):
@@ -179,27 +181,25 @@
     left = dot_split(halves(last[:, :half]), halves(other))
     right = dot_split(halves(last[:, half:]), halves(own))
     natural = (left[:, :half], left[:, half:], right[:, :half], right[:, half:])
-    pair_columns, core_columns, *rest = arranged(parity, natural)
-    high_ref[...], low_ref[...] = halves(beside(pair_columns, core_columns))
-    partial_ref[...] = dot_split(halves(beside(*rest)), halves(above(core_own[...], pair_own[...])))
-
-
-def apply_kernel(high_ref, low_ref, pair_in, core_in, partial_ref, *outputs):
+    order = arranged(parity, natural)
+    high_ref[...], low_ref[...] = halves(beside(*order[: 4 - known]))
+    rows = above(*(ref[...] for ref in inputs))
+    partial_ref[...] = dot_split(halves(beside(*order[4 - known :])), halves(rows))
+
+
+def apply_kernel(high_ref, low_ref, pair_in, core_in, partial_ref, core_out, pair_out):
+    half = core_out.shape[0]
     total = dot_split((high_ref[...], low_ref[...]), halves(above(pair_in[...], core_in[...]))) + partial_ref[...]
-    at = 0
-    for ref in outputs:
-        ref[...] = total[at : at + ref.shape[0]]
-        at += ref.shape[0]
-
-
-def last_kernel(high_ref, low_ref, pair_in, core_in, partial_ref, out_ref, result, sems):
-    columns = pair_in.shape[1]
-    chunk = columns // sems.shape[0]
+    core_out[...] = total[:half]
+    pair_out[...] = total[half:]
+
+
+def last_kernel(high_ref, low_ref, pair_in, partial_ref, out_ref, result, sems):
+    chunk = pair_in.shape[1] // sems.shape[0]
     copies = []
     for number in range(sems.shape[0]):
         at = pl.ds(number * chunk, chunk)
-        far = halves(above(pair_in[:, at], core_in[:, at]))
-        result[:, at] = dot_split((high_ref[...], low_ref[...]), far) + partial_ref[:, at]
+        result[:, at] = dot_split((high_ref[...], low_ref[...]), halves(pair_in[:, at])) + partial_ref[:, at]
         copies.append(pltpu.make_async_copy(result.at[:, at], out_ref.at[:, at], sems.at[number]))
         copies[-1].start()
     for copy in copies:
@@ -270,7 +270,7 @@
     kernel = functools.partial(first_kernel, groups)
     for_core, for_pair, *here = call(kernel, (smem, vmem, vmem), [block, block, *handed], scratch)(place, recv, eigvecs)
 
-    def operators(number, for_exchange, for_core, for_pair):
+    def operators(number, for_exchange, *known):
         if paired:
             sources = (here[0], there[0]) if number == 0 else (here[0], there[0], here[1], there[1])
             if number == 0:
@@ -280,26 +280,27 @@
         else:
             sources = (recv,)
             odd, even = (((0, 1 + 3 * number),), ((0, 2 + 3 * number),)), ((0, 3 + 3 * number),)
-        kernel = functools.partial(operator_kernel, odd, even, for_exchange)
-        weight = ((rows_dev, rows_dev), BF16)
-        inputs = (place, *sources, for_core, for_pair)
+        kernel = functools.partial(operator_kernel, odd, even, for_exchange, len(known))
+        weight = ((rows_dev, half * (4 - len(known))), BF16)
+        inputs = (place, *sources, *known)
         return call(kernel, (smem,) + (vmem,) * (len(inputs) - 1), [whole, weight, weight])(*inputs)
 
     def exchange(number, for_core, for_pair):
         from_pair = lax.ppermute(for_pair, "row", pair_route)
         if paired:
             there.append(lax.ppermute(here[number], "col", [(0, 1), (1, 0)]))
-            for_core, there[number] = lax.optimization_barrier((for_core, there[number]))
+            if number == 0:
+                for_core, there[number] = lax.optimization_barrier((for_core, there[number]))
         return from_pair, lax.ppermute(for_core, "row", core_route)
 
     there = []
-    received = exchange(0, for_core, for_pair)
+    from_pair, from_core = exchange(0, for_core, for_pair)
     partial, high, low = operators(0, True, for_core, for_pair)
-    for_core, for_pair = call(apply_kernel, (vmem,) * 5, [block] * 2)(high, low, *received, partial)
-    received = exchange(1, for_core, for_pair)
-    partial, high, low = operators(1, False, for_core, for_pair)
-    chunks = [vmem(*whole), pltpu.SemaphoreType.DMA((4 if cols_dev % 512 == 0 else 1,))]
-    return call(last_kernel, (vmem,) * 5, [whole], chunks, pl.ANY)(high, low, *received, partial)[0]
+    for_core, for_pair = call(apply_kernel, (vmem,) * 5, [block] * 2)(high, low, from_pair, from_core, partial)
+    from_pair, from_core = exchange(1, for_core, for_pair)
+    partial, high, low = operators(1, False, from_core, for_core, for_pair)
+    chunks = [vmem(*whole), pltpu.SemaphoreType.DMA((OUT_CHUNKS if cols_dev % (128 * OUT_CHUNKS) == 0 else 1,))]
+    return call(last_kernel, (vmem,) * 4, [whole], chunks, pltpu.HBM)(high, low, from_pair, partial)[0]
 
 
 def solution(mesh):

time: 73.2 us -> 73.1 us (level)
    ppermute x2, waiting for transfers between devices: 8.9 us -> 4.66 us  [exchange(): from_pair = lax.ppermute(for_pair, 'row', pair_route)]
    ppermute x2, waiting for transfers between devices: 6.23 us -> 10.1 us  [exchange(): there.append(lax.ppermute(here[number], 'col', [(0, 1), (1, 0)]))]
  transfers between devices with their start and end apart: 6 -> 6, of which waited for: 3 -> 4; matrix products, arithmetic and copies ran while one was open for 0% -> 0% of each run, Pallas kernels for 14% -> 13%
where the time goes in v3:
time: 73.1 us; the launch traced here: 72.9 us
  blocking collectives  36.9 us (50%)
  Pallas kernels  15.7 us (21%)
  waiting for transfers between devices  14.7 us (20%)
  starting transfers between devices  4.49 us (6%)
  local copies, waits for them, and re-layouts  0.94 us (1%)
    all_to_all x1, blocking collectives, on_device(): recv = lax.all_to_all(flat, ('row', 'col'), 0, 0, tiled=True).reshape(shape)  18.9 us
    all_to_all x1, blocking collectives, on_device(): pieces = lax.all_to_all(split, 'row', 0, 0, tiled=True)  17.9 us
    ppermute x2, waiting for transfers between devices, exchange(): there.append(lax.ppermute(here[number], 'col', [(0, 1), (1, 0)]))  10.1 us
    pallas_call x2, Pallas kernels, operators(): call(kernel, (smem,) + (vmem,) * (len(inputs) - 1), [whole, weight, weight])  9.66 us
    ppermute x2, waiting for transfers between devices, exchange(): from_pair = lax.ppermute(for_pair, 'row', pair_route)  4.66 us
    ppermute x2, starting transfers between devices, exchange(): from_pair = lax.ppermute(for_pair, 'row', pair_route)  3.8 us
    pallas_call x1, Pallas kernels, on_device(): call(kernel, (smem, vmem, vmem), [block, block, *handed], scratch)  3.36 us
  transfers between devices with their start and end apart: 6, of which 4 were waited for; matrix products, arithmetic and copies ran while one was open for 0% of the time, Pallas kernels for 13%

profile of v3, /device:TPU:1, one launch (start us, length us, event | category | flops | bytes accessed | tf_op | source)
XLA Modules:
  0.0 72.9 jit_solution(15062948286211295597)
XLA Ops:
  0.0 0.0 copy-start
  0.0 0.1 pad_add_fusion.place_ref
  0.1 0.9 %copy-done = f32[5,1,128,128]{3,2,1,0:T(8,128)S(1)} copy-done((f32[5,1,128,128]{3,2,1,0:T(8,128)S(1)}, f32[5,1,128,128]{3,2,1,0:T(8,128)}, u32[]{:S(2)}) %copy-start) | copy-done | bytes 327704
  1.0 0.0 copy-start.2
  1.0 0.0 copy-start.3
  1.0 17.9 %all_to_all.10.pieces_ref = f32[16,5,8,128]{3,2,1,0:T(8,128)S(1)} all-to-all(f32[16,5,8,128]{3,2,1,0:T(8,128)S(1)} %copy_bitcast_fusion), channel_id=1, replica_groups=mesh['row'=16,'col'=2] {'row'}, dimensions={0} | all-to-all | bytes 655360 | tf_op jit(solution)/shard_map/all_to_all | solution.py:234
  18.9 0.0 copy-done.2
  18.9 0.0 copy-done.3
  18.9 0.0 copy-start.1
  18.9 0.8 %shard_map.46 = f32[16,2,4,8,128]{4,3,2,1,0:T(8,128)S(1)} custom-call(s32[5]{0:T(128)S(1)} %copy-done.3, s32[5,16]{1,0:T(8,128)S(1)} %copy-done.2, f32[16,5,8,128]{3,2,1,0:T(8,128)S(1)} %all_to_all.10.pieces_ref), custom_call_target="tpu_custom_call" | custom-call | tf_op jit(solution)/shard_map/pallas_call | solution.py:258
  19.8 18.9 %all_to_all.11 = f32[32,4,8,128]{3,2,1,0:T(8,128)S(1)} all-to-all(f32[32,4,8,128]{3,2,1,0:T(8,128)S(1)} %bitcast.10), channel_id=1, replica_groups=mesh['row'=16,'col'=2] {'row','col'}, dimensions={0} | all-to-all | bytes 1048576 | tf_op jit(solution)/shard_map/all_to_all | solution.py:264
  38.7 0.0 copy-done.1
  38.7 3.4 %shard_map.47 = (f32[128,1024]{1,0:T(8,128)S(1)}, f32[128,1024]{1,0:T(8,128)S(1)}, f32[16,2,2,8,128]{4,3,2,1,0:T(8,128)S(1)}, f32[16,2,1,8,128]{4,3,2,1,0:T(8,128)S(1)}) custom-call(s32[2]{0:T(128)S(1)} %pad_add_fusion.place_ref, f32[16,2,4,8,128]{4,3,2,1,0:T(8,128)S(1)} %bitcast.9, f32[256,1024]{1,0:T(8,128)S(1)} %copy-done.1), custom_call_target="tpu_custom_call" | custom-call | tf_op jit(solution)/shard_map/pallas_call | solution.py:271
  42.1 0.1 collective-permute-start
  42.2 2.0 %collective-permute-start.2 = (f32[128,1024]{1,0:T(8,128)S(1)}, f32[128,1024]{1,0:T(8,128)S(1)}, u32[]{:S(2)}, u32[]{:S(2)}) collective-permute-start(f32[128,1024]{1,0:T(8,128)S(1)} %get-tuple-element.27.refs_3_), channel_id=1, source_target_pairs={{0,30},{2,4},{4,2},{6,8},{8,6},{10,12},{12,10},{14,16},{16,14},{18... | collective-permute-start | bytes 1572872 | tf_op jit(solution)/shard_map/ppermute | solution.py:289
  44.1 6.2 %collective-permute-done.refs_1_ = f32[16,2,2,8,128]{4,3,2,1,0:T(8,128)S(1)} collective-permute-done((f32[16,2,2,8,128]{4,3,2,1,0:T(8,128)S(1)}, f32[16,2,2,8,128]{4,3,2,1,0:T(8,128)S(1)}, u32[]{:S(2)}, u32[]{:S(2)}) %collective-permute-start) | collective-permute-done | bytes 262176 | tf_op jit(solution)/shard_map/ppermute | solution.py:291
  50.4 0.3 collective-permute-start.3
  50.7 4.7 %shard_map.48 = (f32[256,1024]{1,0:T(8,128)S(1)}, bf16[256,256]{1,0:T(8,128)(2,1)S(1)}, bf16[256,256]{1,0:T(8,128)(2,1)S(1)}) custom-call(s32[2]{0:T(128)S(1)} %pad_add_fusion.place_ref, f32[16,2,2,8,128]{4,3,2,1,0:T(8,128)S(1)} %get-tuple-element.23.refs_0_, f32[16,2,2,8,128]{4,3,2,1,0:T(8,128)S(1)} %collective-permute-done.refs_1_, ...), custom_call_target="tpu_custom_call" | custom-call | tf_op jit(solution)/shard_map/pallas_call | solution.py:286
  55.4 1.3 %collective-permute-done.2.pair_in = f32[128,1024]{1,0:T(8,128)S(1)} collective-permute-done((f32[128,1024]{1,0:T(8,128)S(1)}, f32[128,1024]{1,0:T(8,128)S(1)}, u32[]{:S(2)}, u32[]{:S(2)}) %collective-permute-start.2) | collective-permute-done | bytes 524320 | tf_op jit(solution)/shard_map/ppermute | solution.py:289
  56.6 0.0 collective-permute-done.3.core_in
  56.6 0.6 shard_map.49
  57.2 0.1 collective-permute-start.4
  57.3 1.8 %collective-permute-start.5 = (f32[128,1024]{1,0:T(8,128)S(1)}, f32[128,1024]{1,0:T(8,128)S(1)}, u32[]{:S(2)}, u32[]{:S(2)}) collective-permute-start(f32[128,1024]{1,0:T(8,128)S(1)} %get-tuple-element.33.refs_6_), channel_id=1, source_target_pairs={{0,30},{2,4},{4,2},{6,8},{8,6},{10,12},{12,10},{14,16},{16,14},{18... | collective-permute-start | bytes 1572872 | tf_op jit(solution)/shard_map/ppermute | solution.py:289
  59.1 0.3 collective-permute-start.1
  59.4 3.9 %collective-permute-done.1.refs_3_ = f32[16,2,1,8,128]{4,3,2,1,0:T(8,128)S(1)} collective-permute-done((f32[16,2,1,8,128]{4,3,2,1,0:T(8,128)S(1)}, f32[16,2,1,8,128]{4,3,2,1,0:T(8,128)S(1)}, u32[]{:S(2)}, u32[]{:S(2)}) %collective-permute-start.1) | collective-permute-done | bytes 131104 | tf_op jit(solution)/shard_map/ppermute | solution.py:291
  63.2 0.0 collective-permute-done.4.refs_4_
  63.2 5.0 %shard_map.50 = (f32[256,1024]{1,0:T(8,128)S(1)}, bf16[256,128]{1,0:T(8,128)(2,1)S(1)}, bf16[256,128]{1,0:T(8,128)(2,1)S(1)}) custom-call(s32[2]{0:T(128)S(1)} %pad_add_fusion.place_ref, f32[16,2,2,8,128]{4,3,2,1,0:T(8,128)S(1)} %get-tuple-element.23.refs_0_, f32[16,2,2,8,128]{4,3,2,1,0:T(8,128)S(1)} %collective-permute-done.refs_1_, ...), custom_call_target="tpu_custom_call" | custom-call | tf_op jit(solution)/shard_map/pallas_call | solution.py:286
  68.2 3.4 %collective-permute-done.5.pair_in = f32[128,1024]{1,0:T(8,128)S(1)} collective-permute-done((f32[128,1024]{1,0:T(8,128)S(1)}, f32[128,1024]{1,0:T(8,128)S(1)}, u32[]{:S(2)}, u32[]{:S(2)}) %collective-permute-start.5) | collective-permute-done | bytes 524320 | tf_op jit(solution)/shard_map/ppermute | solution.py:289
  71.6 1.3 %shard_map.51 = f32[256,1024]{1,0:T(8,128)} custom-call(bf16[256,128]{1,0:T(8,128)(2,1)S(1)} %get-tuple-element.34.high_ref, bf16[256,128]{1,0:T(8,128)(2,1)S(1)} %get-tuple-element.35.low_ref, f32[128,1024]{1,0:T(8,128)S(1)} %collective-permute-done.5.pair_in, f32[256,1024]{1,0:T(8,128)S(1)} %get-tuple-element.36.partial_ref), custom_call_target="tpu_custom_call" | custom-call | tf_op jit(solution)/shard_map/pallas_call | solution.py:303
  (1 shorter events, 0.0 us)
Async XLA Ops:
  0.0 1.0 %copy-start = (f32[5,1,128,128]{3,2,1,0:T(8,128)S(1)}, f32[5,1,128,128]{3,2,1,0:T(8,128)}, u32[]{:S(2)}) copy-start(f32[5,1,128,128]{3,2,1,0:T(8,128)} %param.5) | copy-start | bytes 983044
  1.0 17.9 %copy-start.2 = (s32[5,16]{1,0:T(8,128)S(1)}, s32[5,16]{1,0:T(8,128)}, u32[]{:S(2)}) copy-start(s32[5,16]{1,0:T(8,128)} %group_ref.1) | copy-start | bytes 964
  1.0 17.9 %copy-start.3 = (s32[5]{0:T(128)S(1)}, s32[5]{0:T(128)}, u32[]{:S(2)}) copy-start(s32[5]{0:T(128)} %shift_ref.1) | copy-start | bytes 64
  18.9 19.8 %copy-start.1 = (f32[256,1024]{1,0:T(8,128)S(1)}, f32[256,1024]{1,0:T(8,128)}, u32[]{:S(2)}) copy-start(f32[256,1024]{1,0:T(8,128)} %z_ref.1) | copy-start | bytes 3145732
  42.1 8.3 %collective-permute-start = (f32[16,2,2,8,128]{4,3,2,1,0:T(8,128)S(1)}, f32[16,2,2,8,128]{4,3,2,1,0:T(8,128)S(1)}, u32[]{:S(2)}, u32[]{:S(2)}) collective-permute-start(f32[16,2,2,8,128]{4,3,2,1,0:T(8,128)S(1)} %get-tuple-element.23.refs_0_), channel_id=1, source_target_pairs={{0,1},{1,0},{2,3},{3,2},{4,5},{5,4},{6,7},{7,6},{8,9},{9,8},{10,11... | collective-permute-start | bytes 786440 | tf_op jit(solution)/shard_map/ppermute | solution.py:291
  42.2 14.5 %collective-permute-start.2 = (f32[128,1024]{1,0:T(8,128)S(1)}, f32[128,1024]{1,0:T(8,128)S(1)}, u32[]{:S(2)}, u32[]{:S(2)}) collective-permute-start(f32[128,1024]{1,0:T(8,128)S(1)} %get-tuple-element.27.refs_3_), channel_id=1, source_target_pairs={{0,30},{2,4},{4,2},{6,8},{8,6},{10,12},{12,10},{14,16},{16,14},{18... | collective-permute-start | bytes 1572872 | tf_op jit(solution)/shard_map/ppermute | solution.py:289
  50.4 6.3 %collective-permute-start.3 = (f32[128,1024]{1,0:T(8,128)S(1)}, f32[128,1024]{1,0:T(8,128)S(1)}, u32[]{:S(2)}, u32[]{:S(2)}) collective-permute-start(f32[128,1024]{1,0:T(8,128)S(1)} %get-tuple-element.30.refs_2_), channel_id=1, source_target_pairs={{0,2},{2,0},{4,6},{6,4},{8,10},{10,8},{12,14},{14,12},{16,18},{18,... | collective-permute-start | bytes 1572872 | tf_op jit(solution)/shard_map/ppermute | solution.py:294
  57.2 6.0 %collective-permute-start.4 = (f32[128,1024]{1,0:T(8,128)S(1)}, f32[128,1024]{1,0:T(8,128)S(1)}, u32[]{:S(2)}, u32[]{:S(2)}) collective-permute-start(f32[128,1024]{1,0:T(8,128)S(1)} %get-tuple-element.32.refs_5_), channel_id=1, source_target_pairs={{0,2},{2,0},{4,6},{6,4},{8,10},{10,8},{12,14},{14,12},{16,18},{18,... | collective-permute-start | bytes 1572872 | tf_op jit(solution)/shard_map/ppermute | solution.py:294
  57.3 14.3 %collective-permute-start.5 = (f32[128,1024]{1,0:T(8,128)S(1)}, f32[128,1024]{1,0:T(8,128)S(1)}, u32[]{:S(2)}, u32[]{:S(2)}) collective-permute-start(f32[128,1024]{1,0:T(8,128)S(1)} %get-tuple-element.33.refs_6_), channel_id=1, source_target_pairs={{0,30},{2,4},{4,2},{6,8},{8,6},{10,12},{12,10},{14,16},{16,14},{18... | collective-permute-start | bytes 1572872 | tf_op jit(solution)/shard_map/ppermute | solution.py:289
  59.1 4.1 %collective-permute-start.1 = (f32[16,2,1,8,128]{4,3,2,1,0:T(8,128)S(1)}, f32[16,2,1,8,128]{4,3,2,1,0:T(8,128)S(1)}, u32[]{:S(2)}, u32[]{:S(2)}) collective-permute-start(f32[16,2,1,8,128]{4,3,2,1,0:T(8,128)S(1)} %get-tuple-element.26.refs_2_), channel_id=1, source_target_pairs={{0,1},{1,0},{2,3},{3,2},{4,5},{5,4},{6,7},{7,6},{8,9},{9,8},{10,11... | collective-permute-start | bytes 393224 | tf_op jit(solution)/shard_map/ppermute | solution.py:291

commit v4 on v3

--- a/solution.py
+++ b/solution.py
@@ -79,8 +79,13 @@
         inv_col = 2.0 / jnp.sum(kept, axis=1, keepdims=True)
         inv_row = 2.0 / jnp.sum(kept, axis=0, keepdims=True)
         first = jnp.where(corner(1), gram * inv_col * inv_row, 0.0)
-        results.append(jnp.where(diagonal, jnp.broadcast_to(inv_row, gram.shape), 0.0) - first)
-    width = 2
+        pairs = jnp.where(diagonal, jnp.broadcast_to(inv_row, gram.shape), 0.0) - first
+        next_col = jnp.sum(first, axis=1, keepdims=True)
+        next_row = jnp.sum(first, axis=0, keepdims=True)
+        block = jnp.where(corner(2), gram, 0.0)
+        left = inv_col * block - next_col * pltpu.roll(block, order - 1, 0)
+        results.append(pairs - (left * inv_row - pltpu.roll(left, 1, 1) * next_row))
+    width = 4
     while width < order:
         if 4 * width <= order:
             mask = ((row // (4 * width)) == (col // (4 * width))) & ((row // width) < (col // width))

time: 73.1 us -> 73 us (level)
  no operation moved by 1% of the time
where the time goes in v4:
time: 73 us; the launch traced here: 72.8 us
  blocking collectives  36.9 us (51%)
  Pallas kernels  15.6 us (21%)
  waiting for transfers between devices  14.7 us (20%)
  starting transfers between devices  4.49 us (6%)
  local copies, waits for them, and re-layouts  0.94 us (1%)
    all_to_all x1, blocking collectives, on_device(): recv = lax.all_to_all(flat, ('row', 'col'), 0, 0, tiled=True).reshape(shape)  18.9 us
    all_to_all x1, blocking collectives, on_device(): pieces = lax.all_to_all(split, 'row', 0, 0, tiled=True)  17.9 us
    ppermute x2, waiting for transfers between devices, exchange(): there.append(lax.ppermute(here[number], 'col', [(0, 1), (1, 0)]))  10.1 us
    pallas_call x2, Pallas kernels, operators(): call(kernel, (smem,) + (vmem,) * (len(inputs) - 1), [whole, weight, weight])  9.7 us
    ppermute x2, waiting for transfers between devices, exchange(): from_pair = lax.ppermute(for_pair, 'row', pair_route)  4.62 us
    ppermute x2, starting transfers between devices, exchange(): from_pair = lax.ppermute(for_pair, 'row', pair_route)  3.8 us
    pallas_call x1, Pallas kernels, on_device(): call(kernel, (smem, vmem, vmem), [block, block, *handed], scratch)  3.24 us
  transfers between devices with their start and end apart: 6, of which 4 were waited for; matrix products, arithmetic and copies ran while one was open for 0% of the time, Pallas kernels for 13%

profile of v4, /device:TPU:1, one launch (start us, length us, event | category | flops | bytes accessed | tf_op | source)
XLA Modules:
  0.0 72.8 jit_solution(16907818776200036005)
XLA Ops:
  0.0 0.0 copy-start
  0.0 0.1 pad_add_fusion.place_ref
  0.1 0.9 %copy-done = f32[5,1,128,128]{3,2,1,0:T(8,128)S(1)} copy-done((f32[5,1,128,128]{3,2,1,0:T(8,128)S(1)}, f32[5,1,128,128]{3,2,1,0:T(8,128)}, u32[]{:S(2)}) %copy-start) | copy-done | bytes 327704
  1.0 0.0 copy-start.2
  1.0 0.0 copy-start.3
  1.0 17.9 %all_to_all.10.pieces_ref = f32[16,5,8,128]{3,2,1,0:T(8,128)S(1)} all-to-all(f32[16,5,8,128]{3,2,1,0:T(8,128)S(1)} %copy_bitcast_fusion), channel_id=1, replica_groups=mesh['row'=16,'col'=2] {'row'}, dimensions={0} | all-to-all | bytes 655360 | tf_op jit(solution)/shard_map/all_to_all | solution.py:239
  18.9 0.0 copy-done.2
  18.9 0.0 copy-done.3
  18.9 0.0 copy-start.1
  18.9 0.8 %shard_map.46 = f32[16,2,4,8,128]{4,3,2,1,0:T(8,128)S(1)} custom-call(s32[5]{0:T(128)S(1)} %copy-done.3, s32[5,16]{1,0:T(8,128)S(1)} %copy-done.2, f32[16,5,8,128]{3,2,1,0:T(8,128)S(1)} %all_to_all.10.pieces_ref), custom_call_target="tpu_custom_call" | custom-call | tf_op jit(solution)/shard_map/pallas_call | solution.py:263
  19.8 18.9 %all_to_all.11 = f32[32,4,8,128]{3,2,1,0:T(8,128)S(1)} all-to-all(f32[32,4,8,128]{3,2,1,0:T(8,128)S(1)} %bitcast.10), channel_id=1, replica_groups=mesh['row'=16,'col'=2] {'row','col'}, dimensions={0} | all-to-all | bytes 1048576 | tf_op jit(solution)/shard_map/all_to_all | solution.py:269
  38.7 0.0 copy-done.1
  38.7 3.2 %shard_map.47 = (f32[128,1024]{1,0:T(8,128)S(1)}, f32[128,1024]{1,0:T(8,128)S(1)}, f32[16,2,2,8,128]{4,3,2,1,0:T(8,128)S(1)}, f32[16,2,1,8,128]{4,3,2,1,0:T(8,128)S(1)}) custom-call(s32[2]{0:T(128)S(1)} %pad_add_fusion.place_ref, f32[16,2,4,8,128]{4,3,2,1,0:T(8,128)S(1)} %bitcast.9, f32[256,1024]{1,0:T(8,128)S(1)} %copy-done.1), custom_call_target="tpu_custom_call" | custom-call | tf_op jit(solution)/shard_map/pallas_call | solution.py:276
  42.0 0.1 collective-permute-start
  42.0 2.0 %collective-permute-start.2 = (f32[128,1024]{1,0:T(8,128)S(1)}, f32[128,1024]{1,0:T(8,128)S(1)}, u32[]{:S(2)}, u32[]{:S(2)}) collective-permute-start(f32[128,1024]{1,0:T(8,128)S(1)} %get-tuple-element.27.refs_3_), channel_id=1, source_target_pairs={{0,30},{2,4},{4,2},{6,8},{8,6},{10,12},{12,10},{14,16},{16,14},{18... | collective-permute-start | bytes 1572872 | tf_op jit(solution)/shard_map/ppermute | solution.py:294
  44.0 6.2 %collective-permute-done.refs_1_ = f32[16,2,2,8,128]{4,3,2,1,0:T(8,128)S(1)} collective-permute-done((f32[16,2,2,8,128]{4,3,2,1,0:T(8,128)S(1)}, f32[16,2,2,8,128]{4,3,2,1,0:T(8,128)S(1)}, u32[]{:S(2)}, u32[]{:S(2)}) %collective-permute-start) | collective-permute-done | bytes 262176 | tf_op jit(solution)/shard_map/ppermute | solution.py:296
  50.3 0.3 collective-permute-start.3
  50.6 4.7 %shard_map.48 = (f32[256,1024]{1,0:T(8,128)S(1)}, bf16[256,256]{1,0:T(8,128)(2,1)S(1)}, bf16[256,256]{1,0:T(8,128)(2,1)S(1)}) custom-call(s32[2]{0:T(128)S(1)} %pad_add_fusion.place_ref, f32[16,2,2,8,128]{4,3,2,1,0:T(8,128)S(1)} %get-tuple-element.23.refs_0_, f32[16,2,2,8,128]{4,3,2,1,0:T(8,128)S(1)} %collective-permute-done.refs_1_, ...), custom_call_target="tpu_custom_call" | custom-call | tf_op jit(solution)/shard_map/pallas_call | solution.py:291
  55.3 1.2 %collective-permute-done.2.pair_in = f32[128,1024]{1,0:T(8,128)S(1)} collective-permute-done((f32[128,1024]{1,0:T(8,128)S(1)}, f32[128,1024]{1,0:T(8,128)S(1)}, u32[]{:S(2)}, u32[]{:S(2)}) %collective-permute-start.2) | collective-permute-done | bytes 524320 | tf_op jit(solution)/shard_map/ppermute | solution.py:294
  56.5 0.0 collective-permute-done.3.core_in
  56.5 0.6 shard_map.49
  57.1 0.1 collective-permute-start.4
  57.2 1.8 %collective-permute-start.5 = (f32[128,1024]{1,0:T(8,128)S(1)}, f32[128,1024]{1,0:T(8,128)S(1)}, u32[]{:S(2)}, u32[]{:S(2)}) collective-permute-start(f32[128,1024]{1,0:T(8,128)S(1)} %get-tuple-element.33.refs_6_), channel_id=1, source_target_pairs={{0,30},{2,4},{4,2},{6,8},{8,6},{10,12},{12,10},{14,16},{16,14},{18... | collective-permute-start | bytes 1572872 | tf_op jit(solution)/shard_map/ppermute | solution.py:294
  59.0 0.3 collective-permute-start.1
  59.3 3.9 %collective-permute-done.1.refs_3_ = f32[16,2,1,8,128]{4,3,2,1,0:T(8,128)S(1)} collective-permute-done((f32[16,2,1,8,128]{4,3,2,1,0:T(8,128)S(1)}, f32[16,2,1,8,128]{4,3,2,1,0:T(8,128)S(1)}, u32[]{:S(2)}, u32[]{:S(2)}) %collective-permute-start.1) | collective-permute-done | bytes 131104 | tf_op jit(solution)/shard_map/ppermute | solution.py:296
  63.1 0.0 collective-permute-done.4.refs_4_
  63.1 5.0 %shard_map.50 = (f32[256,1024]{1,0:T(8,128)S(1)}, bf16[256,128]{1,0:T(8,128)(2,1)S(1)}, bf16[256,128]{1,0:T(8,128)(2,1)S(1)}) custom-call(s32[2]{0:T(128)S(1)} %pad_add_fusion.place_ref, f32[16,2,2,8,128]{4,3,2,1,0:T(8,128)S(1)} %get-tuple-element.23.refs_0_, f32[16,2,2,8,128]{4,3,2,1,0:T(8,128)S(1)} %collective-permute-done.refs_1_, ...), custom_call_target="tpu_custom_call" | custom-call | tf_op jit(solution)/shard_map/pallas_call | solution.py:291
  68.1 3.4 %collective-permute-done.5.pair_in = f32[128,1024]{1,0:T(8,128)S(1)} collective-permute-done((f32[128,1024]{1,0:T(8,128)S(1)}, f32[128,1024]{1,0:T(8,128)S(1)}, u32[]{:S(2)}, u32[]{:S(2)}) %collective-permute-start.5) | collective-permute-done | bytes 524320 | tf_op jit(solution)/shard_map/ppermute | solution.py:294
  71.5 1.3 %shard_map.51 = f32[256,1024]{1,0:T(8,128)} custom-call(bf16[256,128]{1,0:T(8,128)(2,1)S(1)} %get-tuple-element.34.high_ref, bf16[256,128]{1,0:T(8,128)(2,1)S(1)} %get-tuple-element.35.low_ref, f32[128,1024]{1,0:T(8,128)S(1)} %collective-permute-done.5.pair_in, f32[256,1024]{1,0:T(8,128)S(1)} %get-tuple-element.36.partial_ref), custom_call_target="tpu_custom_call" | custom-call | tf_op jit(solution)/shard_map/pallas_call | solution.py:308
  (1 shorter events, 0.0 us)
Async XLA Ops:
  0.0 1.0 %copy-start = (f32[5,1,128,128]{3,2,1,0:T(8,128)S(1)}, f32[5,1,128,128]{3,2,1,0:T(8,128)}, u32[]{:S(2)}) copy-start(f32[5,1,128,128]{3,2,1,0:T(8,128)} %param.5) | copy-start | bytes 983044
  1.0 17.9 %copy-start.2 = (s32[5,16]{1,0:T(8,128)S(1)}, s32[5,16]{1,0:T(8,128)}, u32[]{:S(2)}) copy-start(s32[5,16]{1,0:T(8,128)} %group_ref.1) | copy-start | bytes 964
  1.0 17.9 %copy-start.3 = (s32[5]{0:T(128)S(1)}, s32[5]{0:T(128)}, u32[]{:S(2)}) copy-start(s32[5]{0:T(128)} %shift_ref.1) | copy-start | bytes 64
  18.9 19.8 %copy-start.1 = (f32[256,1024]{1,0:T(8,128)S(1)}, f32[256,1024]{1,0:T(8,128)}, u32[]{:S(2)}) copy-start(f32[256,1024]{1,0:T(8,128)} %z_ref.1) | copy-start | bytes 3145732
  42.0 8.3 %collective-permute-start = (f32[16,2,2,8,128]{4,3,2,1,0:T(8,128)S(1)}, f32[16,2,2,8,128]{4,3,2,1,0:T(8,128)S(1)}, u32[]{:S(2)}, u32[]{:S(2)}) collective-permute-start(f32[16,2,2,8,128]{4,3,2,1,0:T(8,128)S(1)} %get-tuple-element.23.refs_0_), channel_id=1, source_target_pairs={{0,1},{1,0},{2,3},{3,2},{4,5},{5,4},{6,7},{7,6},{8,9},{9,8},{10,11... | collective-permute-start | bytes 786440 | tf_op jit(solution)/shard_map/ppermute | solution.py:296
  42.0 14.5 %collective-permute-start.2 = (f32[128,1024]{1,0:T(8,128)S(1)}, f32[128,1024]{1,0:T(8,128)S(1)}, u32[]{:S(2)}, u32[]{:S(2)}) collective-permute-start(f32[128,1024]{1,0:T(8,128)S(1)} %get-tuple-element.27.refs_3_), channel_id=1, source_target_pairs={{0,30},{2,4},{4,2},{6,8},{8,6},{10,12},{12,10},{14,16},{16,14},{18... | collective-permute-start | bytes 1572872 | tf_op jit(solution)/shard_map/ppermute | solution.py:294
  50.3 6.3 %collective-permute-start.3 = (f32[128,1024]{1,0:T(8,128)S(1)}, f32[128,1024]{1,0:T(8,128)S(1)}, u32[]{:S(2)}, u32[]{:S(2)}) collective-permute-start(f32[128,1024]{1,0:T(8,128)S(1)} %get-tuple-element.30.refs_2_), channel_id=1, source_target_pairs={{0,2},{2,0},{4,6},{6,4},{8,10},{10,8},{12,14},{14,12},{16,18},{18,... | collective-permute-start | bytes 1572872 | tf_op jit(solution)/shard_map/ppermute | solution.py:299
  57.1 6.0 %collective-permute-start.4 = (f32[128,1024]{1,0:T(8,128)S(1)}, f32[128,1024]{1,0:T(8,128)S(1)}, u32[]{:S(2)}, u32[]{:S(2)}) collective-permute-start(f32[128,1024]{1,0:T(8,128)S(1)} %get-tuple-element.32.refs_5_), channel_id=1, source_target_pairs={{0,2},{2,0},{4,6},{6,4},{8,10},{10,8},{12,14},{14,12},{16,18},{18,... | collective-permute-start | bytes 1572872 | tf_op jit(solution)/shard_map/ppermute | solution.py:299
  57.2 14.3 %collective-permute-start.5 = (f32[128,1024]{1,0:T(8,128)S(1)}, f32[128,1024]{1,0:T(8,128)S(1)}, u32[]{:S(2)}, u32[]{:S(2)}) collective-permute-start(f32[128,1024]{1,0:T(8,128)S(1)} %get-tuple-element.33.refs_6_), channel_id=1, source_target_pairs={{0,30},{2,4},{4,2},{6,8},{8,6},{10,12},{12,10},{14,16},{16,14},{18... | collective-permute-start | bytes 1572872 | tf_op jit(solution)/shard_map/ppermute | solution.py:294
  59.0 4.1 %collective-permute-start.1 = (f32[16,2,1,8,128]{4,3,2,1,0:T(8,128)S(1)}, f32[16,2,1,8,128]{4,3,2,1,0:T(8,128)S(1)}, u32[]{:S(2)}, u32[]{:S(2)}) collective-permute-start(f32[16,2,1,8,128]{4,3,2,1,0:T(8,128)S(1)} %get-tuple-element.26.refs_2_), channel_id=1, source_target_pairs={{0,1},{1,0},{2,3},{3,2},{4,5},{5,4},{6,7},{7,6},{8,9},{9,8},{10,11... | collective-permute-start | bytes 393224 | tf_op jit(solution)/shard_map/ppermute | solution.py:296
